TPU v7x, 256 devices: a whole 4x4x8 slice. The times are simulated.
256 devices in a mesh: row: 16 (over y, z_lo, core), col: 16 (over x, z_hi).
Axes of the slice: x: 4, y: 4, z: 8 (z_hi: 4, z_lo: 2; z = z_hi * 2 + z_lo), core: 2. Of those that a mesh axis runs over, the one named last changes fastest.
Arguments:
- features: bfloat16 [65536, 512], P('col', 'row'), may hold values from -6 to 6
- weight: bfloat16 [512, 512], replicated, may hold values from -0.25 to 0.25
- degrees: int32 [65536], replicated, may hold values from 4 to 64
- tile_values: bfloat16 [16, 16, 128, 128, 128], P('row', 'col'), may hold values from 0 to 1
- tile_row: int32 [16, 16, 128], P('row', 'col'), may hold values from 0 to 31
- tile_col: int32 [16, 16, 128], P('row', 'col'), may hold values from 0 to 31
- tile_count: int32 [16, 16], P('row', 'col'), may hold values from 16 to 128, as said below
- cotangent: bfloat16 [65536, 512], P('row', 'col'), may hold values from -6 to 6
Outputs:
- output: bfloat16 [65536, 512], P('row', 'col')
- grad_features: bfloat16 [65536, 512], P('col', 'row')
- grad_weight: float32 [512, 512], P(None, 'row')
Inputs may be any that keep to these rules, and one draw needn't show every extreme that they name: tile_count equals 128 on some device in every draw.
All inputs are finite; a program needn't handle non-finite values.
Results may differ from a plain program's by a relative error of at most 0.03.
Values may be sent and summed in bfloat16 or wider, within the bound.
A program may use at most 128 MiB of HBM per device.

v0:
```python
import math

import jax
import jax.numpy as jnp
from jax import lax
from jax.sharding import PartitionSpec as P

TILE = 128


def tile_apply(tiles, gather_of, target_of, count, dense, blocks_out, form):
    slots = tiles.shape[0]
    group = math.gcd(slots, 16)
    width = dense.shape[1]
    stacked = dense.reshape(-1, TILE, width)
    target = jnp.where(jnp.arange(slots) < count, target_of, blocks_out)
    tile_groups = tiles.reshape(slots // group, group, TILE, TILE)
    gather_groups = gather_of.reshape(slots // group, group)
    target_groups = target.reshape(slots // group, group)

    def accumulate(total, items):
        block_tiles, block_gather, block_target = items
        pieces = stacked[block_gather]
        product = jnp.einsum(form, block_tiles, pieces, preferred_element_type=jnp.float32)
        return (total + jax.ops.segment_sum(product, block_target, num_segments=blocks_out), None)

    start = jnp.zeros((blocks_out, TILE, width), jnp.float32)
    total, unused = lax.scan(accumulate, start, (tile_groups, gather_groups, target_groups))
    return total.reshape(blocks_out * TILE, width)


def shards(features, weight, degrees, tile_values, tile_row, tile_col, tile_count, cotangent):
    row_index = lax.axis_index("row")
    col_index = lax.axis_index("col")
    row_count = lax.axis_size("row")
    col_count = lax.axis_size("col")
    tiles = tile_values[0, 0]
    rows_of = tile_row[0, 0]
    cols_of = tile_col[0, 0]
    count = tile_count[0, 0]
    col_span = features.shape[0]
    own_rows = col_span // row_count
    row_span = own_rows * col_count
    scale_all = lax.rsqrt(degrees.astype(jnp.float32))
    row_scale = lax.dynamic_slice_in_dim(scale_all, row_index * row_span, row_span, 0)
    col_scale = lax.dynamic_slice_in_dim(scale_all, col_index * col_span, col_span, 0)
    whole_x = lax.all_gather(features, "row", axis=1, tiled=True)
    projected = (
        jnp.dot(whole_x, weight, preferred_element_type=jnp.float32) * col_scale[:, None]
    ).astype(jnp.bfloat16)
    partial_value = tile_apply(
        tiles, cols_of, rows_of, count, projected, row_span // TILE, "tab,tbf->taf"
    )
    summed = lax.psum_scatter(
        partial_value.astype(jnp.bfloat16), "col", scatter_dimension=1, tiled=True
    ).astype(jnp.float32)
    hidden_in = summed * row_scale[:, None]
    output = jax.nn.silu(hidden_in).astype(jnp.bfloat16)
    sigma = jax.nn.sigmoid(hidden_in)
    grad_in = (
        cotangent.astype(jnp.float32)
        * sigma
        * (1.0 + hidden_in * (1.0 - sigma))
        * row_scale[:, None]
    ).astype(jnp.bfloat16)
    grad_rows = lax.all_gather(grad_in, "col", axis=1, tiled=True)
    backward = tile_apply(
        tiles, rows_of, cols_of, count, grad_rows, col_span // TILE, "tab,taf->tbf"
    )
    back_sum = lax.psum_scatter(
        backward.astype(jnp.bfloat16), "row", scatter_dimension=1, tiled=True
    ).astype(jnp.float32)
    grad_part = (back_sum * col_scale[:, None]).astype(jnp.bfloat16)
    grad_block = lax.all_gather(grad_part, "row", axis=1, tiled=True)
    width = features.shape[1]
    weight_rows = lax.dynamic_slice_in_dim(weight, row_index * width, width, 0)
    grad_features = lax.dot_general(
        grad_block, weight_rows, (((1,), (1,)), ((), ())), preferred_element_type=jnp.float32
    ).astype(jnp.bfloat16)
    local_weight = lax.dot_general(
        whole_x, grad_part, (((0,), (0,)), ((), ())), preferred_element_type=jnp.float32
    )
    grad_weight = lax.psum(local_weight.astype(jnp.bfloat16), "col").astype(jnp.float32)
    return (output, grad_features, grad_weight)


def solution(mesh):
    in_specs = (
        P("col", "row"),
        P(),
        P(),
        P("row", "col", None, None, None),
        P("row", "col", None),
        P("row", "col", None),
        P("row", "col"),
        P("row", "col"),
    )
    out_specs = (P("row", "col"), P("col", "row"), P(None, "row"))
    return jax.shard_map(shards, mesh=mesh, in_specs=in_specs, out_specs=out_specs, check_vma=False)
```

profile of v0, /device:TPU:0, one launch (start us, length us, event | category | flops | bytes accessed | tf_op | source)
XLA Modules:
  0.0 700.2 jit_solution(15603399696895497912)
XLA Ops:
  13.0 38.2 %all-gather.4.cloned.1.call-done = bf16[4096,512]{0,1:T(8,128)(2,1)} async-done(((bf16[4096,32]{0,1:T(8,128)(2,1)}), bf16[4096,512]{0,1:T(8,128)(2,1)}) %all-gather.4.cloned.1.call-update) | async-done | bytes 4194320 | tf_op jit(solution)/shard_map/all_gather | solution.py:47
  51.1 6.5 multiply_convert_fusion
  57.6 4.3 broadcast.58.clone
  61.9 118.5 %while.20 = (s32[]{:T(128)}, f32[32,128,512]{2,1,0:T(8,128)}, s32[8,16]{1,0:T(8,128)S(1)}, bf16[8,16,128,128]{3,2,1,0:T(8,128)(2,1)}, s32[8,16]{1,0:T(8,128)S(1)}, /*index=5*/bf16[32,128,512]{2,1,0:T(8,128)(2,1)}, s32[]{:T(128)}) while((s32[]{:T(128)}, f32[32,128,512]{2,1,0:T(8,128)}, s32[8,16]{1,0:T(8,128)S(1)}, ...), condition=%wide.region_2.3_spmd, body=%wide.region_0.2_spmd.sunk | while | flops 269485120 | bytes 23597600 | solution.py:28
  68.5 9.6 %scatter_fusion = f32[32,128,512]{2,1,0:T(8,128)} fusion(f32[32,128,512]{2,1,0:T(8,128)} %get-tuple-element.203, s32[16]{0:T(128)S(1)} %fusion.39, f32[16,128,512]{2,1,0:T(8,128)} %fusion.41), kind=kCustom, calls=%fused_computation.2.clone.1 | custom fusion | flops 1048576 | bytes 12582976 | tf_op jit(solution)/shard_map/while/body/eval_jaxpr/scatter-add | solution.py:25
  84.7 9.3 %scatter_fusion = f32[32,128,512]{2,1,0:T(8,128)} fusion(f32[32,128,512]{2,1,0:T(8,128)} %get-tuple-element.203, s32[16]{0:T(128)S(1)} %fusion.39, f32[16,128,512]{2,1,0:T(8,128)} %fusion.41), kind=kCustom, calls=%fused_computation.2.clone.1 | custom fusion | flops 1048576 | bytes 12582976 | tf_op jit(solution)/shard_map/while/body/eval_jaxpr/scatter-add | solution.py:25
  100.6 7.8 %scatter_fusion = f32[32,128,512]{2,1,0:T(8,128)} fusion(f32[32,128,512]{2,1,0:T(8,128)} %get-tuple-element.203, s32[16]{0:T(128)S(1)} %fusion.39, f32[16,128,512]{2,1,0:T(8,128)} %fusion.41), kind=kCustom, calls=%fused_computation.2.clone.1 | custom fusion | flops 1048576 | bytes 12582976 | tf_op jit(solution)/shard_map/while/body/eval_jaxpr/scatter-add | solution.py:25
  115.0 7.8 %scatter_fusion = f32[32,128,512]{2,1,0:T(8,128)} fusion(f32[32,128,512]{2,1,0:T(8,128)} %get-tuple-element.203, s32[16]{0:T(128)S(1)} %fusion.39, f32[16,128,512]{2,1,0:T(8,128)} %fusion.41), kind=kCustom, calls=%fused_computation.2.clone.1 | custom fusion | flops 1048576 | bytes 12582976 | tf_op jit(solution)/shard_map/while/body/eval_jaxpr/scatter-add | solution.py:25
  129.4 7.8 %scatter_fusion = f32[32,128,512]{2,1,0:T(8,128)} fusion(f32[32,128,512]{2,1,0:T(8,128)} %get-tuple-element.203, s32[16]{0:T(128)S(1)} %fusion.39, f32[16,128,512]{2,1,0:T(8,128)} %fusion.41), kind=kCustom, calls=%fused_computation.2.clone.1 | custom fusion | flops 1048576 | bytes 12582976 | tf_op jit(solution)/shard_map/while/body/eval_jaxpr/scatter-add | solution.py:25
  143.8 7.8 %scatter_fusion = f32[32,128,512]{2,1,0:T(8,128)} fusion(f32[32,128,512]{2,1,0:T(8,128)} %get-tuple-element.203, s32[16]{0:T(128)S(1)} %fusion.39, f32[16,128,512]{2,1,0:T(8,128)} %fusion.41), kind=kCustom, calls=%fused_computation.2.clone.1 | custom fusion | flops 1048576 | bytes 12582976 | tf_op jit(solution)/shard_map/while/body/eval_jaxpr/scatter-add | solution.py:25
  158.3 7.8 %scatter_fusion = f32[32,128,512]{2,1,0:T(8,128)} fusion(f32[32,128,512]{2,1,0:T(8,128)} %get-tuple-element.203, s32[16]{0:T(128)S(1)} %fusion.39, f32[16,128,512]{2,1,0:T(8,128)} %fusion.41), kind=kCustom, calls=%fused_computation.2.clone.1 | custom fusion | flops 1048576 | bytes 12582976 | tf_op jit(solution)/shard_map/while/body/eval_jaxpr/scatter-add | solution.py:25
  172.7 7.8 %scatter_fusion = f32[32,128,512]{2,1,0:T(8,128)} fusion(f32[32,128,512]{2,1,0:T(8,128)} %get-tuple-element.203, s32[16]{0:T(128)S(1)} %fusion.39, f32[16,128,512]{2,1,0:T(8,128)} %fusion.41), kind=kCustom, calls=%fused_computation.2.clone.1 | custom fusion | flops 1048576 | bytes 12582976 | tf_op jit(solution)/shard_map/while/body/eval_jaxpr/scatter-add | solution.py:25
  180.5 6.0 convert_element_type.50
  186.4 6.4 copy.21
  192.9 106.0 %reduce-scatter.5.cloned.1.call-done = bf16[4096,32]{0,1:T(8,128)(2,1)} async-done(((bf16[4096,512]{0,1:T(8,128)(2,1)}), bf16[4096,32]{0,1:T(8,128)(2,1)}) %reduce-scatter.5.cloned.1.call-update) | async-done | bytes 262160 | tf_op jit(solution)/shard_map/reduce_scatter | solution.py:54
  301.0 6.4 copy.15
  307.4 67.2 %all-gather.6.cloned.1.call-done = bf16[4096,512]{0,1:T(8,128)(2,1)} async-done(((bf16[4096,32]{0,1:T(8,128)(2,1)}), bf16[4096,512]{0,1:T(8,128)(2,1)}) %all-gather.6.cloned.1.call-update) | async-done | bytes 4194320 | tf_op jit(solution)/shard_map/all_gather | solution.py:66
  374.6 6.5 copy.22
  381.1 4.3 broadcast.58
  385.4 119.0 %while.21 = (s32[]{:T(128)}, f32[32,128,512]{2,1,0:T(8,128)}, s32[8,16]{1,0:T(8,128)S(1)}, bf16[8,16,128,128]{2,3,1,0:T(8,128)(2,1)}, s32[8,16]{1,0:T(8,128)S(1)}, /*index=5*/bf16[32,128,512]{2,1,0:T(8,128)(2,1)}, s32[]{:T(128)}) while((s32[]{:T(128)}, f32[32,128,512]{2,1,0:T(8,128)}, s32[8,16]{1,0:T(8,128)S(1)}, ...), condition=%wide.region_6.7_spmd, body=%wide.region_4.6_spmd.sunk | while | flops 269485120 | bytes 23597600 | solution.py:28
  392.0 9.4 %scatter_fusion.1 = f32[32,128,512]{2,1,0:T(8,128)} fusion(f32[32,128,512]{2,1,0:T(8,128)} %get-tuple-element.224, s32[16]{0:T(128)S(1)} %fusion.44, f32[16,128,512]{2,1,0:T(8,128)} %fusion.46), kind=kCustom, calls=%fused_computation.3.clone.1 | custom fusion | flops 1048576 | bytes 12582976 | tf_op jit(solution)/shard_map/while/body/eval_jaxpr/scatter-add | solution.py:25
  408.0 9.4 %scatter_fusion.1 = f32[32,128,512]{2,1,0:T(8,128)} fusion(f32[32,128,512]{2,1,0:T(8,128)} %get-tuple-element.224, s32[16]{0:T(128)S(1)} %fusion.44, f32[16,128,512]{2,1,0:T(8,128)} %fusion.46), kind=kCustom, calls=%fused_computation.3.clone.1 | custom fusion | flops 1048576 | bytes 12582976 | tf_op jit(solution)/shard_map/while/body/eval_jaxpr/scatter-add | solution.py:25
  424.0 7.8 %scatter_fusion.1 = f32[32,128,512]{2,1,0:T(8,128)} fusion(f32[32,128,512]{2,1,0:T(8,128)} %get-tuple-element.224, s32[16]{0:T(128)S(1)} %fusion.44, f32[16,128,512]{2,1,0:T(8,128)} %fusion.46), kind=kCustom, calls=%fused_computation.3.clone.1 | custom fusion | flops 1048576 | bytes 12582976 | tf_op jit(solution)/shard_map/while/body/eval_jaxpr/scatter-add | solution.py:25
  438.5 7.8 %scatter_fusion.1 = f32[32,128,512]{2,1,0:T(8,128)} fusion(f32[32,128,512]{2,1,0:T(8,128)} %get-tuple-element.224, s32[16]{0:T(128)S(1)} %fusion.44, f32[16,128,512]{2,1,0:T(8,128)} %fusion.46), kind=kCustom, calls=%fused_computation.3.clone.1 | custom fusion | flops 1048576 | bytes 12582976 | tf_op jit(solution)/shard_map/while/body/eval_jaxpr/scatter-add | solution.py:25
  453.0 7.8 %scatter_fusion.1 = f32[32,128,512]{2,1,0:T(8,128)} fusion(f32[32,128,512]{2,1,0:T(8,128)} %get-tuple-element.224, s32[16]{0:T(128)S(1)} %fusion.44, f32[16,128,512]{2,1,0:T(8,128)} %fusion.46), kind=kCustom, calls=%fused_computation.3.clone.1 | custom fusion | flops 1048576 | bytes 12582976 | tf_op jit(solution)/shard_map/while/body/eval_jaxpr/scatter-add | solution.py:25
  467.5 7.8 %scatter_fusion.1 = f32[32,128,512]{2,1,0:T(8,128)} fusion(f32[32,128,512]{2,1,0:T(8,128)} %get-tuple-element.224, s32[16]{0:T(128)S(1)} %fusion.44, f32[16,128,512]{2,1,0:T(8,128)} %fusion.46), kind=kCustom, calls=%fused_computation.3.clone.1 | custom fusion | flops 1048576 | bytes 12582976 | tf_op jit(solution)/shard_map/while/body/eval_jaxpr/scatter-add | solution.py:25
  482.0 7.8 %scatter_fusion.1 = f32[32,128,512]{2,1,0:T(8,128)} fusion(f32[32,128,512]{2,1,0:T(8,128)} %get-tuple-element.224, s32[16]{0:T(128)S(1)} %fusion.44, f32[16,128,512]{2,1,0:T(8,128)} %fusion.46), kind=kCustom, calls=%fused_computation.3.clone.1 | custom fusion | flops 1048576 | bytes 12582976 | tf_op jit(solution)/shard_map/while/body/eval_jaxpr/scatter-add | solution.py:25
  496.5 7.8 %scatter_fusion.1 = f32[32,128,512]{2,1,0:T(8,128)} fusion(f32[32,128,512]{2,1,0:T(8,128)} %get-tuple-element.224, s32[16]{0:T(128)S(1)} %fusion.44, f32[16,128,512]{2,1,0:T(8,128)} %fusion.46), kind=kCustom, calls=%fused_computation.3.clone.1 | custom fusion | flops 1048576 | bytes 12582976 | tf_op jit(solution)/shard_map/while/body/eval_jaxpr/scatter-add | solution.py:25
  504.4 6.0 convert_element_type.56
  510.4 6.4 copy.23
  517.0 83.5 %reduce-scatter.7.cloned.1.call-done = bf16[32,4096]{1,0:T(8,128)(2,1)} async-done(((bf16[512,4096]{1,0:T(8,128)(2,1)}), bf16[32,4096]{1,0:T(8,128)(2,1)}) %reduce-scatter.7.cloned.1.call-update) | async-done | bytes 262160
  607.2 82.1 %psum.7 = bf16[512,32]{0,1:T(8,128)(2,1)S(1)} all-reduce(bf16[512,32]{0,1:T(8,128)(2,1)S(1)} %fusion.14), channel_id=1, replica_groups=mesh['row'=16,'col'=16] {'col'}, use_global_device_ids=true, to_apply=%region_8.9 | all-reduce | flops 16384 | bytes 65536 | tf_op jit(solution)/shard_map/psum | solution.py:83
  (111 shorter events, 123.9 us)
Async XLA Ops:
  7.2 44.0 %copy-start = (bf16[512,512]{1,0:T(8,128)(2,1)S(1)}, bf16[512,512]{1,0:T(8,128)(2,1)}, u32[]{:S(2)}) copy-start(bf16[512,512]{1,0:T(8,128)(2,1)} %param.13) | copy-start | bytes 1572868
  7.2 43.9 %all-gather.4.cloned.1.call-start = ((), (), s32[]{:S(2)}) async-start(), calls=%async_computation.2 | async-start | bytes 4456448 | tf_op jit(solution)/shard_map/all_gather | solution.py:47
  7.9 291.0 %reduce-scatter.5.cloned.1.call-start = ((), (), s32[]{:S(2)}) async-start(), calls=%async_computation.3 | async-start | bytes 4456448 | tf_op jit(solution)/shard_map/reduce_scatter | solution.py:54
  192.8 106.1 %copy-start.1 = (bf16[4096,32]{0,1:T(8,128)(2,1)S(1)}, bf16[4096,32]{0,1:T(8,128)(2,1)}, u32[]{:S(2)}) copy-start(bf16[4096,32]{0,1:T(8,128)(2,1)} %param.19) | copy-start | bytes 786436
  192.9 181.8 %all-gather.6.cloned.1.call-start = ((), (), s32[]{:S(2)}) async-start(), calls=%async_computation.4 | async-start | bytes 4456448 | tf_op jit(solution)/shard_map/all_gather | solution.py:66
  301.0 299.5 %reduce-scatter.7.cloned.1.call-start = ((), (), s32[]{:S(2)}) async-start(), calls=%async_computation.6 | async-start | bytes 4456448
  516.8 173.2 %all-gather.8.cloned.1.call-start = ((), (), s32[]{:S(2)}) async-start(), calls=%async_computation.5 | async-start | bytes 4456448 | tf_op jit(solution)/shard_map/all_gather | solution.py:74
Sparse Core Ops, SparseCore 0:
  9.9 41.2 all-gather.3
  193.0 105.9 reduce-scatter.4
  302.3 72.3 all-gather.5
  516.9 83.5 reduce-scatter.6
  603.8 38.2 all-gather.7
where the time goes:
time: 703 us; the launch traced here: 700 us
  waiting for transfers between devices  296 us (42%)
  other arithmetic  151 us (21%)
  local copies, waits for them, and re-layouts  83.4 us (12%)
  blocking collectives  82.1 us (12%)
  matrix products  72.9 us (10%)
  between operations  14.5 us (2%)
    scatter-add x16, other arithmetic, accumulate(): jax.ops.segment_sum(product, block_target, num_segments=blocks_out)  132 us
    reduce_scatter x1, waiting for transfers between devices, shards(): lax.psum_scatter(partial_value.astype(jnp.bfloat16), 'col', scatter_dimen...  106 us
    unnamed x6, waiting for transfers between devices  84.2 us
    psum x1, blocking collectives, shards(): lax.psum(local_weight.astype(jnp.bfloat16), 'col').astype(jnp.float32)  82.1 us
    all_gather x1, waiting for transfers between devices, shards(): grad_rows = lax.all_gather(grad_in, 'col', axis=1, tiled=True)  67.2 us
    dot_general x16, matrix products, accumulate(): jnp.einsum(form, block_tiles, pieces, preferred_element_type=jnp.float32)  59.1 us
    gather x16, local copies, waits for them, and re-layouts, accumulate(): pieces = stacked[block_gather]  45.9 us
    all_gather x1, waiting for transfers between devices, shards(): whole_x = lax.all_gather(features, 'row', axis=1, tiled=True)  38.2 us
  transfers between devices with their start and end apart: 5, of which 4 were waited for; matrix products, arithmetic and copies ran while one was open for 2% of the time, Pallas kernels for 0%

commit v1 on v0

v1 whole, which is shorter than its diff:
```python
import functools

import jax
import jax.numpy as jnp
from jax import lax
from jax.experimental import pallas as pl
from jax.experimental.pallas import tpu as pltpu
from jax.sharding import PartitionSpec as P

TILE = 128
N_Y, N_ZL, N_CORE = 4, 2, 2
N_X, N_ZH = 4, 4
VMEM_BYTES = 60 * 1024 * 1024
BF16, F32 = jnp.bfloat16, jnp.float32
MESH = pl.DeviceIdType.MESH


class Links:
    def __init__(self, send_sems, recv_sems):
        self.send_sems, self.recv_sems, self.used, self.open = send_sems, recv_sems, 0, []

    def start(self, src, dst, device):
        copy = pltpu.make_async_remote_copy(
            src_ref=src,
            dst_ref=dst,
            send_sem=self.send_sems.at[self.used],
            recv_sem=self.recv_sems.at[self.used],
            device_id=device,
            device_id_type=MESH,
        )
        self.used += 1
        copy.start()
        self.open.append(copy)
        return copy

    def drain(self):
        for copy in self.open:
            copy.wait_send()


def greet(peers):
    barrier = pltpu.get_barrier_semaphore()
    for peer in peers:
        pl.semaphore_signal(barrier, inc=1, device_id=peer, device_id_type=MESH)
    pl.semaphore_wait(barrier, len(peers))


def pipeline(stages, chunks):
    for step in range(chunks + len(stages) - 1):
        for stage in range(len(stages)):
            if 0 <= step - stage < chunks:
                stages[stage](step - stage)


def row_peers():
    g, h = lax.axis_index("row"), lax.axis_index("col")
    y, zl, core = g // (N_ZL * N_CORE), (g // N_CORE) % N_ZL, g % N_CORE

    def at(y_of, zl_of, core_of):
        return (y_of * N_ZL + zl_of) * N_CORE + core_of

    return g, h, y, zl, core, at


def add(left, right):
    return (left.astype(F32) + right.astype(F32)).astype(BF16)


AG_CHUNKS = 4
AG_SENDS = 17


def project_kernel(x_ref, wt_ref, scale_ref, all_ref, proj_ref, send_sems, recv_sems):
    links = Links(send_sems, recv_sems)
    g, h, y, zl, core, at = row_peers()
    up, down, far = (y + 1) % N_Y, (y + N_Y - 1) % N_Y, (y + 2) % N_Y
    zp = 1 - zl
    right, left = (at(up, zl, core), h), (at(down, zl, core), h)
    z_peer, c_peer = (at(y, zp, core), h), (at(y, zl, 1 - core), h)
    greet([right, left, z_peer, c_peer])
    span = x_ref.shape[1] // AG_CHUNKS
    depth = x_ref.shape[0]
    half = depth // 2
    all_ref[g] = x_ref[...]
    sent = {}

    def lanes(q):
        return pl.ds(q * span, span)

    def block(owner, q, rows=slice(None)):
        return all_ref.at[owner, rows, lanes(q)]

    def forward(owner, q, device, rows=slice(None)):
        return links.start(block(owner, q, rows), block(owner, q, rows), device)

    first, second = pl.ds(0, half), pl.ds(half, half)

    def stage_own(q):
        src = x_ref.at[:, lanes(q)]
        for name, device in (("z", z_peer), ("r", right), ("l", left), ("c0", c_peer)):
            sent[name, q] = links.start(src, block(g, q), device)

    def stage_z(q):
        sent["z", q].wait_recv()
        owner = at(y, zp, core)
        for name, device in (("zr", right), ("zl", left), ("c1", c_peer)):
            sent[name, q] = forward(owner, q, device)

    def stage_y(q):
        sent["r", q].wait_recv()
        sent["fr", q] = forward(at(down, zl, core), q, right, first)
        sent["l", q].wait_recv()
        sent["fl", q] = forward(at(up, zl, core), q, left, second)
        sent["c2", q] = forward(at(down, zl, core), q, c_peer)
        sent["c3", q] = forward(at(up, zl, core), q, c_peer)

    def stage_zy(q):
        sent["zr", q].wait_recv()
        sent["gr", q] = forward(at(down, zp, core), q, right, first)
        sent["zl", q].wait_recv()
        sent["gl", q] = forward(at(up, zp, core), q, left, second)
        sent["c4", q] = forward(at(down, zp, core), q, c_peer)
        sent["c5", q] = forward(at(up, zp, core), q, c_peer)

    def stage_far(q):
        sent["fr", q].wait_recv()
        sent["fl", q].wait_recv()
        sent["c6", q] = forward(at(far, zl, core), q, c_peer)
        sent["gr", q].wait_recv()
        sent["gl", q].wait_recv()
        sent["c7", q] = forward(at(far, zp, core), q, c_peer)

    def stage_project(q):
        for i in range(8):
            sent["c%d" % i, q].wait_recv()
        wide = min(span, 256)

        @pl.loop(0, span // wide)
        def one(j):
            where = pl.ds(pl.multiple_of(q * span + j * wide, wide), wide)
            x = all_ref[:, :, where].reshape(-1, wide)
            value = jnp.dot(wt_ref[...], x, preferred_element_type=F32)
            proj_ref[:, where] = (value * scale_ref[:, where]).astype(BF16)

    pipeline([stage_own, stage_z, stage_y, stage_zy, stage_far, stage_project], AG_CHUNKS)
    links.drain()


def gather_project(x, wt, scale):
    depth, span = x.shape
    hidden = wt.shape[0]
    vmem = pl.BlockSpec(memory_space=pltpu.VMEM)
    count = AG_CHUNKS * AG_SENDS
    return pl.pallas_call(
        project_kernel,
        out_shape=(
            jax.ShapeDtypeStruct((N_Y * N_ZL * N_CORE, depth, span), BF16),
            jax.ShapeDtypeStruct((hidden, span), BF16),
        ),
        in_specs=[vmem] * 3,
        out_specs=(vmem, vmem),
        scratch_shapes=[pltpu.SemaphoreType.DMA((count,)), pltpu.SemaphoreType.DMA((count,))],
        compiler_params=pltpu.CompilerParams(
            collective_id=0, has_side_effects=True, vmem_limit_bytes=VMEM_BYTES
        ),
        name="gather_project",
    )(x, wt, scale)


GROUP = 4


def spmm_kernel(transpose, gather_ref, target_ref, count_ref, tiles_ref, dense_ref, out_ref, acc_ref):
    blocks = out_ref.shape[1] // TILE
    contract = (((1,), (1,)), ((), ())) if transpose else (((1,), (0,)), ((), ()))

    @pl.loop(0, blocks)
    def clear(j):
        acc_ref[:, pl.ds(pl.multiple_of(j * TILE, TILE), TILE)] = jnp.zeros(
            (acc_ref.shape[0], TILE), F32
        )

    count = count_ref[0]

    @pl.loop(0, (count + GROUP - 1) // GROUP)
    def step(i):
        products, targets = [], []
        for j in range(GROUP):
            t = i * GROUP + j
            source = pl.multiple_of(gather_ref[t] * TILE, TILE)
            products.append(
                lax.dot_general(
                    dense_ref[:, pl.ds(source, TILE)],
                    tiles_ref[t],
                    contract,
                    preferred_element_type=F32,
                )
            )
            place = jnp.where(t < count, target_ref[t], blocks)
            targets.append(pl.multiple_of(place * TILE, TILE))
        for product, place in zip(products, targets):
            acc_ref[:, pl.ds(place, TILE)] += product

    @pl.loop(0, blocks)
    def finish(j):
        where = pl.ds(pl.multiple_of(j * TILE, TILE), TILE)
        out_ref[:, where] = acc_ref[:, where].astype(BF16)


def spmm(transpose, gather_of, target_of, count, tiles, dense):
    smem = pl.BlockSpec(memory_space=pltpu.SMEM)
    vmem = pl.BlockSpec(memory_space=pltpu.VMEM)
    hidden, span = dense.shape
    return pl.pallas_call(
        functools.partial(spmm_kernel, transpose),
        out_shape=jax.ShapeDtypeStruct((hidden, span), BF16),
        in_specs=[smem, smem, smem, vmem, vmem],
        out_specs=vmem,
        scratch_shapes=[pltpu.VMEM((hidden, span + TILE), F32)],
        compiler_params=pltpu.CompilerParams(vmem_limit_bytes=VMEM_BYTES),
        name="spmm_t" if transpose else "spmm",
    )(gather_of, target_of, count, tiles, dense)


MID_CHUNKS = 4
MID_SENDS = 4 + 2 + 3 + 3 + 2 + 2


def middle_kernel(
    part_ref, cot_ref, scale_ref, grad_ref, out_ref,
    in_ref, merge_ref, sum_ref, z_ref, send_sems, recv_sems,
):
    links = Links(send_sems, recv_sems)
    g, h = lax.axis_index("row"), lax.axis_index("col")
    x, zh = h // N_ZH, h % N_ZH
    up, down, far = (x + 1) % N_X, (x + N_X - 1) % N_X, (x + 2) % N_X
    right, left = (g, up * N_ZH + zh), (g, down * N_ZH + zh)
    z_peers = [(g, x * N_ZH + (zh + d) % N_ZH) for d in range(1, N_ZH)]
    greet([right, left] + z_peers)
    nodes = part_ref.shape[1]
    span = nodes // MID_CHUNKS
    own = cot_ref.shape[0]
    group = own * N_ZH
    half = group // 2
    sent = {}

    def lanes(q):
        return pl.ds(q * span, span)

    def part(x_of, side, q):
        start = pl.multiple_of(x_of * group + side * half, half)
        return part_ref.at[pl.ds(start, half), lanes(q)]

    def slot(i, q):
        return in_ref.at[i, :, lanes(q)]

    def reduce_out(q):
        sent["f0", q] = links.start(part(far, 0, q), slot(0, q), right)
        sent["f1", q] = links.start(part(far, 1, q), slot(1, q), left)
        sent["d0", q] = links.start(part(up, 1, q), slot(2, q), right)
        sent["d1", q] = links.start(part(down, 0, q), slot(3, q), left)

    def reduce_merge(q):
        sent["f0", q].wait_recv()
        merge_ref[0, :, lanes(q)] = add(slot(0, q)[...], part(up, 0, q)[...])
        sent["m0", q] = links.start(merge_ref.at[0, :, lanes(q)], slot(4, q), right)
        sent["f1", q].wait_recv()
        merge_ref[1, :, lanes(q)] = add(slot(1, q)[...], part(down, 1, q)[...])
        sent["m1", q] = links.start(merge_ref.at[1, :, lanes(q)], slot(5, q), left)

    def reduce_z(q):
        for name in ("d0", "d1", "m0", "m1"):
            sent[name, q].wait_recv()
        for side, (merged, direct) in enumerate(((4, 3), (5, 2))):
            total = slot(merged, q)[...].astype(F32) + slot(direct, q)[...].astype(F32)
            total = total + part(x, side, q)[...].astype(F32)
            sum_ref[pl.ds(side * half, half), lanes(q)] = total.astype(BF16)
        for d in range(1, N_ZH):
            rows = pl.ds(pl.multiple_of(((zh + d) % N_ZH) * own, own), own)
            sent["z", d, q] = links.start(
                sum_ref.at[rows, lanes(q)], z_ref.at[d - 1, :, lanes(q)], z_peers[d - 1]
            )

    def activate(q):
        value = sum_ref[pl.ds(pl.multiple_of(zh * own, own), own), lanes(q)].astype(F32)
        for d in range(1, N_ZH):
            sent["z", d, q].wait_recv()
            value = value + z_ref[d - 1, :, lanes(q)].astype(F32)
        scale = scale_ref[:, lanes(q)]
        hidden = value * scale
        sigma = 1.0 / (1.0 + jnp.exp(-hidden))
        out_ref[:, lanes(q)] = (hidden * sigma).astype(BF16)
        grad = cot_ref[:, lanes(q)].astype(F32) * sigma * (1.0 + hidden * (1.0 - sigma)) * scale
        grad_ref[h, :, lanes(q)] = grad.astype(BF16)
        mine = grad_ref.at[h, :, lanes(q)]
        for d in range(1, N_ZH):
            sent["g", d, q] = links.start(mine, mine, z_peers[d - 1])

    def gather_x(q):
        for d in range(1, N_ZH):
            sent["g", d, q].wait_recv()
        mine = grad_ref.at[pl.ds(x * N_ZH, N_ZH), :, lanes(q)]
        sent["gr", q] = links.start(mine, mine, right)
        sent["gl", q] = links.start(mine, mine, left)

    def gather_far(q):
        sent["gr", q].wait_recv()
        first = grad_ref.at[pl.ds(down * N_ZH, N_ZH // 2), :, lanes(q)]
        sent["hr", q] = links.start(first, first, right)
        sent["gl", q].wait_recv()
        second = grad_ref.at[pl.ds(up * N_ZH + N_ZH // 2, N_ZH // 2), :, lanes(q)]
        sent["hl", q] = links.start(second, second, left)

    def gather_end(q):
        sent["hr", q].wait_recv()
        sent["hl", q].wait_recv()

    pipeline(
        [reduce_out, reduce_merge, reduce_z, activate, gather_x, gather_far, gather_end],
        MID_CHUNKS,
    )
    links.drain()


def middle(part, cot, scale):
    hidden, span = part.shape
    own = cot.shape[0]
    half = own * N_ZH // 2
    vmem = pl.BlockSpec(memory_space=pltpu.VMEM)
    count = MID_CHUNKS * MID_SENDS
    return pl.pallas_call(
        middle_kernel,
        out_shape=(
            jax.ShapeDtypeStruct((N_X * N_ZH, own, span), BF16),
            jax.ShapeDtypeStruct((own, span), BF16),
        ),
        in_specs=[vmem] * 3,
        out_specs=(vmem, vmem),
        scratch_shapes=[
            pltpu.VMEM((6, half, span), BF16),
            pltpu.VMEM((2, half, span), BF16),
            pltpu.VMEM((2 * half, span), BF16),
            pltpu.VMEM((N_ZH - 1, own, span), BF16),
            pltpu.SemaphoreType.DMA((count,)),
            pltpu.SemaphoreType.DMA((count,)),
        ],
        compiler_params=pltpu.CompilerParams(
            collective_id=1, has_side_effects=True, vmem_limit_bytes=VMEM_BYTES
        ),
        name="middle",
    )(part, cot, scale)


END_CHUNKS = 4
END_SENDS = 1 + 4 + 2 + 1


def final_kernel(
    back_ref, x_ref, w_ref, scale_ref, gf_ref, gw_ref,
    core_ref, half_ref, in_ref, merge_ref, sum_ref, z_ref, gp_ref, gft_ref, gpa_ref,
    lw_ref, px_ref, pz_ref, send_sems, recv_sems,
):
    links = Links(send_sems, recv_sems)
    g, h, y, zl, core, at = row_peers()
    rows_in_all = N_Y * N_ZL * N_CORE
    x, zh = h // N_ZH, h % N_ZH
    up, down, far = (y + 1) % N_Y, (y + N_Y - 1) % N_Y, (y + 2) % N_Y
    zp = 1 - zl
    right, left = (at(up, zl, core), h), (at(down, zl, core), h)
    z_peer, c_peer = (at(y, zp, core), h), (at(y, zl, 1 - core), h)
    row_group = [((g + d) % rows_in_all, h) for d in range(1, rows_in_all)]
    x_group = [(g, ((x + d) % N_X) * N_ZH + zh) for d in range(1, N_X)]
    zh_group = [(g, x * N_ZH + (zh + d) % N_ZH) for d in range(1, N_ZH)]
    greet(row_group + x_group + zh_group)
    hidden, nodes = back_ref.shape
    rows = hidden // END_CHUNKS
    mine = nodes // rows_in_all
    side_nodes = nodes // N_CORE
    y_nodes = mine * N_ZL
    half = rows // 2
    sent = {}

    def chunk(q, start=0, size=rows):
        return pl.ds(q * rows + start, size)

    def core_out(q):
        there = pl.ds(pl.multiple_of((1 - core) * side_nodes, side_nodes), side_nodes)
        sent["c", q] = links.start(back_ref.at[chunk(q), there], core_ref.at[chunk(q), :], c_peer)

    def y_part(y_of, side, q):
        lanes = pl.ds(pl.multiple_of(y_of * y_nodes, y_nodes), y_nodes)
        return half_ref.at[chunk(q, side * half, half), lanes]

    def slot(i, q):
        return in_ref.at[i, pl.ds(q * half, half), :]

    def y_out(q):
        sent["c", q].wait_recv()
        wide = min(side_nodes, 512)

        @pl.loop(0, side_nodes // wide)
        def one(j):
            offset = pl.multiple_of(j * wide, wide)
            there = pl.ds(pl.multiple_of(core * side_nodes + j * wide, wide), wide)
            half_ref[chunk(q), pl.ds(offset, wide)] = add(
                back_ref[chunk(q), there], core_ref[chunk(q), pl.ds(offset, wide)]
            )

        sent["f0", q] = links.start(y_part(far, 0, q), slot(0, q), right)
        sent["f1", q] = links.start(y_part(far, 1, q), slot(1, q), left)
        sent["d0", q] = links.start(y_part(up, 1, q), slot(2, q), right)
        sent["d1", q] = links.start(y_part(down, 0, q), slot(3, q), left)

    def y_merge(q):
        sent["f0", q].wait_recv()
        merge_ref[0, pl.ds(q * half, half), :] = add(slot(0, q)[...], y_part(up, 0, q)[...])
        sent["m0", q] = links.start(merge_ref.at[0, pl.ds(q * half, half), :], slot(4, q), right)
        sent["f1", q].wait_recv()
        merge_ref[1, pl.ds(q * half, half), :] = add(slot(1, q)[...], y_part(down, 1, q)[...])
        sent["m1", q] = links.start(merge_ref.at[1, pl.ds(q * half, half), :], slot(5, q), left)

    def z_out(q):
        for name in ("d0", "d1", "m0", "m1"):
            sent[name, q].wait_recv()
        for side, (merged, direct) in enumerate(((4, 3), (5, 2))):
            total = slot(merged, q)[...].astype(F32) + slot(direct, q)[...].astype(F32)
            total = total + y_part(y, side, q)[...].astype(F32)
            sum_ref[chunk(q, side * half, half), :] = total.astype(BF16)
        there = pl.ds(pl.multiple_of(zp * mine, mine), mine)
        sent["z", q] = links.start(sum_ref.at[chunk(q), there], z_ref.at[chunk(q), :], z_peer)

    def scaled(q):
        sent["z", q].wait_recv()
        here = pl.ds(pl.multiple_of(zl * mine, mine), mine)
        value = sum_ref[chunk(q), here].astype(F32) + z_ref[chunk(q), :].astype(F32)
        gp_ref[chunk(q), :] = (value * scale_ref[...]).astype(BF16)

    pipeline([core_out, y_out, y_merge, z_out, scaled], END_CHUNKS)

    own = hidden // rows_in_all
    place = pl.ds(pl.multiple_of(core * side_nodes + (y * N_ZL + zl) * mine, mine), mine)

    def spread(src_ref, dst_ref):
        copies = []
        for d in range(1, rows_in_all):
            other = pl.ds(pl.multiple_of(((g + d) % rows_in_all) * own, own), own)
            copies.append(links.start(src_ref.at[other, :], dst_ref.at[:, place], row_group[d - 1]))
        dst_ref[:, place] = src_ref[pl.ds(pl.multiple_of(g * own, own), own), :]
        return copies

    grads = spread(gp_ref, gpa_ref)
    gft_ref[...] = jnp.dot(w_ref[...], gp_ref[...], preferred_element_type=F32).astype(BF16)
    outs = spread(gft_ref, gf_ref)
    for copy in grads:
        copy.wait_recv()
    feats = x_ref.shape[0]
    wide = min(nodes, 512)
    total = jnp.zeros((own, feats), F32)
    for j in range(nodes // wide):
        where = pl.ds(j * wide, wide)
        total = total + lax.dot_general(
            gpa_ref[:, where], x_ref[:, where], (((1,), (1,)), ((), ())), preferred_element_type=F32
        )

    def share(total, buffer, index, group):
        lw_ref[index] = total.astype(BF16)
        copies = [
            links.start(lw_ref.at[index], buffer.at[i], peer) for i, peer in enumerate(group)
        ]
        for i, copy in enumerate(copies):
            copy.wait_recv()
            total = total + buffer[i].astype(F32)
        return total

    total = share(total, px_ref, 0, x_group)
    gw_ref[...] = share(total, pz_ref, 1, zh_group)
    for copy in outs:
        copy.wait_recv()
    links.drain()


def final(back, x_all, w, scale):
    hidden, span = back.shape
    feats = x_all.shape[0]
    rows_in_all = N_Y * N_ZL * N_CORE
    own = hidden // rows_in_all
    mine = span // rows_in_all
    vmem = pl.BlockSpec(memory_space=pltpu.VMEM)
    count = END_CHUNKS * END_SENDS + 2 * (rows_in_all - 1) + (N_X - 1) + (N_ZH - 1)
    y_nodes = mine * N_ZL
    return pl.pallas_call(
        final_kernel,
        out_shape=(
            jax.ShapeDtypeStruct((own, span), BF16),
            jax.ShapeDtypeStruct((own, feats), F32),
        ),
        in_specs=[vmem] * 4,
        out_specs=(vmem, vmem),
        scratch_shapes=[
            pltpu.VMEM((hidden, span // N_CORE), BF16),
            pltpu.VMEM((hidden, span // N_CORE), BF16),
            pltpu.VMEM((6, hidden // 2, y_nodes), BF16),
            pltpu.VMEM((2, hidden // 2, y_nodes), BF16),
            pltpu.VMEM((hidden, y_nodes), BF16),
            pltpu.VMEM((hidden, mine), BF16),
            pltpu.VMEM((hidden, mine), BF16),
            pltpu.VMEM((feats, mine), BF16),
            pltpu.VMEM((own, span), BF16),
            pltpu.VMEM((2, own, feats), BF16),
            pltpu.VMEM((N_X - 1, own, feats), BF16),
            pltpu.VMEM((N_ZH - 1, own, feats), BF16),
            pltpu.SemaphoreType.DMA((count,)),
            pltpu.SemaphoreType.DMA((count,)),
        ],
        compiler_params=pltpu.CompilerParams(
            collective_id=2, has_side_effects=True, vmem_limit_bytes=VMEM_BYTES
        ),
        name="final",
    )(back, x_all, w, scale)


def shards(features, weight, degrees, tile_values, tile_row, tile_col, tile_count, cotangent):
    g = lax.axis_index("row")
    h = lax.axis_index("col")
    tiles, rows_of, cols_of = tile_values[0, 0], tile_row[0, 0], tile_col[0, 0]
    count = tile_count[0]
    nodes = features.shape[0]
    scale_of = lambda start, size: lax.rsqrt(
        lax.dynamic_slice_in_dim(degrees, start, size, 0).astype(F32)
    )[None, :]
    col_scale = scale_of(h * nodes, nodes)
    row_scale = scale_of(g * nodes, nodes)
    mine = nodes // (N_Y * N_ZL * N_CORE)
    place = (g % N_CORE) * (nodes // N_CORE) + (g // N_CORE) * mine
    mine_scale = scale_of(h * nodes + place, mine)
    x_all, projected = gather_project(features.T, weight.T, col_scale)
    part = spmm(True, cols_of, rows_of, count, tiles, projected)
    grad_in, output = middle(part, cotangent.T, row_scale)
    back = spmm(False, rows_of, cols_of, count, tiles, grad_in.reshape(part.shape))
    grad_features, grad_weight = final(
        back, x_all.reshape(-1, nodes), weight, mine_scale
    )
    return (output.T, grad_features.T, grad_weight.T)


def solution(mesh):
    in_specs = (
        P("col", "row"),
        P(),
        P(),
        P("row", "col", None, None, None),
        P("row", "col", None),
        P("row", "col", None),
        P("row", "col"),
        P("row", "col"),
    )
    out_specs = (P("row", "col"), P("col", "row"), P(None, "row"))
    return jax.shard_map(shards, mesh=mesh, in_specs=in_specs, out_specs=out_specs, check_vma=False)
```

time: 703 us -> 233 us (0.33)
  waiting for transfers between devices: 296 us -> 0 us
  Pallas kernels: 0 us -> 221 us
  other arithmetic: 151 us -> 2.74 us
  blocking collectives: 82.1 us -> 0 us
  local copies, waits for them, and re-layouts: 83.4 us -> 5.95 us
  matrix products: 72.9 us -> 0 us
  between operations: 14.5 us -> 1.34 us
    pallas_call x0 -> x5, Pallas kernels: none -> 221 us  [the longest x1 99.8 us: middle(): pl.pallas_call(middle_kernel, out_shape=(jax.ShapeDtypeStruct((N_X * N_ZH...]
    scatter-add x16 -> x0, other arithmetic: 132 us -> none  [accumulate(): jax.ops.segment_sum(product, block_target, num_segments=blocks_out)]
    reduce_scatter x1 -> x0, waiting for transfers between devices: 106 us -> none  [shards(): lax.psum_scatter(partial_value.astype(jnp.bfloat16), 'col', scatter_dimen...]
    all_gather x3 -> x0, waiting for transfers between devices: 105 us -> none  [the longest x1 67.2 us: shards(): grad_rows = lax.all_gather(grad_in, 'col', axis=1, tiled=True)]
    unnamed x6 -> x0, waiting for transfers between devices: 84.2 us -> none
    psum x1 -> x0, blocking collectives: 82.1 us -> none  [shards(): lax.psum(local_weight.astype(jnp.bfloat16), 'col').astype(jnp.float32)]
    dot_general x19 -> x0, matrix products: 72.9 us -> none  [the longest x16 59.1 us: accumulate(): jnp.einsum(form, block_tiles, pieces, preferred_element_type=jnp.float32)]
    gather x16 -> x0, local copies, waits for them, and re-layouts: 45.9 us -> none  [accumulate(): pieces = stacked[block_gather]]
  transfers between devices with their start and end apart: 5 -> 0, of which waited for: 4 -> 0; matrix products, arithmetic and copies ran while one was open for 2% -> 0% of each run, Pallas kernels for 0% -> 0%
where the time goes in v1:
time: 233 us; the launch traced here: 231 us
  Pallas kernels  221 us (95%)
  local copies, waits for them, and re-layouts  5.95 us (3%)
  other arithmetic  2.74 us (1%)
    pallas_call x1, Pallas kernels, middle(): pl.pallas_call(middle_kernel, out_shape=(jax.ShapeDtypeStruct((N_X * N_ZH...  99.8 us
    pallas_call x1, Pallas kernels, final(): pl.pallas_call(final_kernel, out_shape=(jax.ShapeDtypeStruct((own, span),...  58.9 us
    pallas_call x1, Pallas kernels, gather_project(): pl.pallas_call(project_kernel, out_shape=(jax.ShapeDtypeStruct((N_Y * N_Z...  32.4 us
    pallas_call x2, Pallas kernels, spmm(): pl.pallas_call(functools.partial(spmm_kernel, transpose), out_shape=jax.S...  30 us
    unnamed x6, local copies, waits for them, and re-layouts  5.95 us

profile of v1, /device:TPU:0, one launch (start us, length us, event | category | flops | bytes accessed | tf_op | source)
XLA Modules:
  0.0 231.2 jit_solution(3477029240819947906)
XLA Ops:
  1.3 1.3 convert_rsqrt_fusion.2
  2.6 1.4 convert_rsqrt_fusion
  4.0 2.1 copy.11
  6.1 32.4 %gather_project.1 = (bf16[16,32,4096]{2,1,0:T(8,128)(2,1)}, bf16[512,4096]{1,0:T(8,128)(2,1)}) custom-call(bf16[32,4096]{1,0:T(8,128)(2,1)} %bitcast.22, bf16[512,512]{1,0:T(8,128)(2,1)} %bitcast.21, f32[1,4096]{1,0:T(1,128)} %bitcast.28), custom_call_target="tpu_custom_call" | custom-call | tf_op jit(solution)/shard_map/gather_project/pallas_call | solution.py:154
  38.5 15.2 %spmm_t.1.part_ref = bf16[512,4096]{1,0:T(8,128)(2,1)} custom-call(s32[128]{0:T(128)} %bitcast.30, s32[128]{0:T(128)} %bitcast.32, s32[1]{0:T(128)} %bitcast.15.count_ref, bf16[128,128,128]{2,1,0:T(8,128)(2,1)} %bitcast.17, bf16[512,4096]{1,0:T(8,128)(2,1)} %get-tuple-element.9.dense_ref), custom_call_target="tpu_custom_call" | custom-call | tf_op jit(solution)/shard_map/spmm_t/pallas_call | solution.py:214
  53.7 99.8 %middle.1 = (bf16[16,32,4096]{2,1,0:T(8,128)(2,1)}, bf16[32,4096]{1,0:T(8,128)(2,1)}) custom-call(bf16[512,4096]{1,0:T(8,128)(2,1)} %spmm_t.1.part_ref, bf16[32,4096]{1,0:T(8,128)(2,1)} %bitcast.23, f32[1,4096]{1,0:T(1,128)} %bitcast.26), custom_call_target="tpu_custom_call" | custom-call | tf_op jit(solution)/shard_map/middle/pallas_call | solution.py:331
  153.5 14.8 %spmm.1.back_ref = bf16[512,4096]{1,0:T(8,128)(2,1)} custom-call(s32[128]{0:T(128)} %bitcast.33, s32[128]{0:T(128)} %bitcast.31, s32[1]{0:T(128)} %bitcast.16.count_ref, bf16[128,128,128]{2,1,0:T(8,128)(2,1)} %bitcast.18, bf16[512,4096]{1,0:T(8,128)(2,1)} %bitcast.20), custom_call_target="tpu_custom_call" | custom-call | tf_op jit(solution)/shard_map/spmm/pallas_call | solution.py:214
  168.4 0.0 copy-start
  168.4 58.9 %final.1 = (bf16[32,4096]{1,0:T(8,128)(2,1)}, f32[32,512]{1,0:T(8,128)}) custom-call(bf16[512,4096]{1,0:T(8,128)(2,1)} %spmm.1.back_ref, bf16[512,4096]{1,0:T(8,128)(2,1)} %bitcast.19, bf16[512,512]{1,0:T(8,128)(2,1)} %w_ref.1, f32[1,256]{1,0:T(1,128)} %bitcast.29), custom_call_target="tpu_custom_call" | custom-call | tf_op jit(solution)/shard_map/final/pallas_call | solution.py:491
  227.3 0.0 copy-done
  227.3 0.7 copy.16
  228.0 1.7 copy.17
  229.7 1.5 copy.18
Async XLA Ops:
  168.4 58.9 %copy-start = (bf16[32,4096]{1,0:T(8,128)(2,1)S(1)}, bf16[32,4096]{1,0:T(8,128)(2,1)}, u32[]{:S(2)}) copy-start(bf16[32,4096]{1,0:T(8,128)(2,1)} %get-tuple-element.10) | copy-start | bytes 786436

commit v2 on v0

v2 whole, which is shorter than its diff:
```python
import jax
import jax.numpy as jnp
from jax import lax
from jax.experimental import pallas as pl
from jax.experimental.pallas import tpu as pltpu
from jax.sharding import PartitionSpec as P

TILE = 128
PARTS = 2
N_Y, N_ZL, N_CORE = 4, 2, 2
N_X, N_ZH = 4, 4
N_ROW, N_COL = N_Y * N_ZL * N_CORE, N_X * N_ZH
AG_CHUNKS = 4
MID_CHUNKS = 4
END_CHUNKS = 2
GROUP = 4
VMEM_BYTES = 60 * 1024 * 1024
BF16, F32, I32 = jnp.bfloat16, jnp.float32, jnp.int32
MESH = pl.DeviceIdType.MESH
SENDS = (
    AG_CHUNKS * 17
    + PARTS * MID_CHUNKS * 16
    + PARTS * END_CHUNKS * 8
    + (PARTS + 1) * (N_ROW - 1)
    + PARTS * (N_X - 1 + N_ZH - 1)
)


class Links:
    def __init__(self, send_sems, recv_sems):
        self.send_sems, self.recv_sems, self.used, self.open = send_sems, recv_sems, 0, []

    def start(self, src, dst, device):
        copy = pltpu.make_async_remote_copy(
            src_ref=src,
            dst_ref=dst,
            send_sem=self.send_sems.at[self.used],
            recv_sem=self.recv_sems.at[self.used],
            device_id=device,
            device_id_type=MESH,
        )
        self.used += 1
        copy.start()
        self.open.append(copy)
        return copy

    def drain(self):
        for copy in self.open:
            copy.wait_send()


def greet(peers):
    barrier = pltpu.get_barrier_semaphore()
    for peer in peers:
        pl.semaphore_signal(barrier, inc=1, device_id=peer, device_id_type=MESH)
    pl.semaphore_wait(barrier, len(peers))


def add(left, right):
    return (left.astype(F32) + right.astype(F32)).astype(BF16)


def sorted_by(key, gather):
    shape = (TILE, TILE)
    i = lax.broadcasted_iota(I32, shape, 0)
    j = lax.broadcasted_iota(I32, shape, 1)
    across = jnp.broadcast_to(key, shape)
    down = across.T
    before = (down < across) | ((down == across) & (i < j))
    rank = jnp.broadcast_to(jnp.sum(before.astype(I32), axis=0, keepdims=True), shape).T

    def total(where, value):
        return jnp.sum(jnp.where(where, value, 0), axis=0, keepdims=True)

    order = total(rank == j, i)
    source = total(rank == j, jnp.broadcast_to(gather, shape).T)
    same = (total(rank == j, down) == total(rank == j - 1, down)).astype(I32)
    last = jnp.maximum(total(down <= j, 1) - 1, 0)
    some = jnp.minimum(total(down == j, 1), 1)
    return [order, source, last, same, some]


def plan_kernel(rows_ref, cols_ref, count_ref, table_ref):
    live = lax.broadcasted_iota(I32, (1, TILE), 1) < count_ref[0, 0]
    rows_of, cols_of = rows_ref[...], cols_ref[...]
    lines = sorted_by(jnp.where(live, rows_of, TILE), cols_of)
    lines += sorted_by(jnp.where(live, cols_of, TILE), rows_of)
    table_ref[...] = jnp.zeros_like(table_ref)
    for i, line in enumerate(lines):
        table_ref[pl.ds(i, 1), :] = line


def kernel(
    x_hbm, w_hbm, deg_hbm, tiles_hbm, idx_ref, table_ref, cot_hbm,
    out_ref, gf_ref, gw_ref,
    all_ref, tiles_ref, w_ref, wt_ref, cot_ref, deg_ref, cs_ref, rs_ref, same_ref, some_ref,
    proj_ref, seg_ref, acc_ref, part_ref,
    in_ref, merge_ref, sum_ref, z_ref, g0_ref, g1_ref, back_ref,
    core_ref, half_ref, yin_ref, ymerge_ref, ysum_ref, zin_ref, gp_ref, gft_ref, gpa_ref,
    lw_ref, px_ref, pz_ref, local_sems, send_sems, recv_sems,
):
    links = Links(send_sems, recv_sems)
    g, h = lax.axis_index("row"), lax.axis_index("col")
    y, zl, core = g // (N_ZL * N_CORE), (g // N_CORE) % N_ZL, g % N_CORE
    x, zh = h // N_ZH, h % N_ZH
    zp = 1 - zl

    def at(y_of, zl_of, core_of):
        return (y_of * N_ZL + zl_of) * N_CORE + core_of

    y_up, y_down, y_far = (y + 1) % N_Y, (y + N_Y - 1) % N_Y, (y + 2) % N_Y
    x_up, x_down, x_far = (x + 1) % N_X, (x + N_X - 1) % N_X, (x + 2) % N_X
    y_right, y_left = (at(y_up, zl, core), h), (at(y_down, zl, core), h)
    x_right, x_left = (g, x_up * N_ZH + zh), (g, x_down * N_ZH + zh)
    z_peer, c_peer = (at(y, zp, core), h), (at(y, zl, 1 - core), h)
    row_group = [((g + d) % N_ROW, h) for d in range(1, N_ROW)]
    x_group = [(g, ((x + d) % N_X) * N_ZH + zh) for d in range(1, N_X)]
    zh_group = [(g, x * N_ZH + (zh + d) % N_ZH) for d in range(1, N_ZH)]

    nodes = x_hbm.shape[1]
    hidden = w_ref.shape[1]
    wide = hidden // PARTS
    depth = x_hbm.shape[0]
    own = depth // PARTS
    blocks = nodes // TILE
    deg_rows = nodes // TILE
    sent = {}

    local = {}
    loads = (
        ("x", x_hbm, all_ref.at[g]),
        ("w", w_hbm, w_ref),
        ("dc", deg_hbm.at[pl.ds(pl.multiple_of(h * deg_rows, deg_rows), deg_rows)], deg_ref.at[0]),
        ("dr", deg_hbm.at[pl.ds(pl.multiple_of(g * deg_rows, deg_rows), deg_rows)], deg_ref.at[1]),
        ("tiles", tiles_hbm, tiles_ref),
        ("cot", cot_hbm, cot_ref),
    )
    for i, (name, src, dst) in enumerate(loads):
        local[name] = pltpu.make_async_copy(src, dst, local_sems.at[i])
        local[name].start()

    greet(row_group + x_group + zh_group)

    ag_span = nodes // AG_CHUNKS
    first, second = pl.ds(0, depth // 2), pl.ds(depth // 2, depth // 2)

    def ag_lanes(q):
        return pl.ds(q * ag_span, ag_span)

    def forward(owner, q, device, rows=slice(None)):
        block = all_ref.at[owner, rows, ag_lanes(q)]
        return links.start(block, block, device)

    def ag_own(q):
        src = x_hbm.at[:, ag_lanes(q)]
        for name, device in (("z", z_peer), ("r", y_right), ("l", y_left), ("c0", c_peer)):
            sent[name, q] = links.start(src, all_ref.at[g, :, ag_lanes(q)], device)

    def ag_z(q):
        sent["z", q].wait_recv()
        owner = at(y, zp, core)
        for name, device in (("zr", y_right), ("zl", y_left), ("c1", c_peer)):
            sent[name, q] = forward(owner, q, device)

    def ag_y(q):
        sent["r", q].wait_recv()
        sent["fr", q] = forward(at(y_down, zl, core), q, y_right, first)
        sent["l", q].wait_recv()
        sent["fl", q] = forward(at(y_up, zl, core), q, y_left, second)
        sent["c2", q] = forward(at(y_down, zl, core), q, c_peer)
        sent["c3", q] = forward(at(y_up, zl, core), q, c_peer)

    def ag_zy(q):
        sent["zr", q].wait_recv()
        sent["gr", q] = forward(at(y_down, zp, core), q, y_right, first)
        sent["zl", q].wait_recv()
        sent["gl", q] = forward(at(y_up, zp, core), q, y_left, second)
        sent["c4", q] = forward(at(y_down, zp, core), q, c_peer)
        sent["c5", q] = forward(at(y_up, zp, core), q, c_peer)

    def ag_far(q):
        sent["fr", q].wait_recv()
        sent["fl", q].wait_recv()
        sent["c6", q] = forward(at(y_far, zl, core), q, c_peer)
        sent["gr", q].wait_recv()
        sent["gl", q].wait_recv()
        sent["c7", q] = forward(at(y_far, zp, core), q, c_peer)

    def project(q):
        for i in range(8):
            sent["c%d" % i, q].wait_recv()
        if q == 0:
            local["x"].wait()
        step = min(ag_span, 256)

        @pl.loop(0, ag_span // step)
        def one(j):
            where = pl.ds(pl.multiple_of(q * ag_span + j * step, step), step)
            block = all_ref[:, :, where].reshape(-1, step)
            for p in range(PARTS):
                value = jnp.dot(
                    wt_ref[pl.ds(p * wide, wide), :], block, preferred_element_type=F32
                )
                proj_ref[p, :, where] = (value * cs_ref[:, where]).astype(BF16)

    def prepare():
        local["w"].wait()
        turned = w_ref[...].T
        for owner in range(N_COL):
            for p in range(PARTS):
                start = owner * depth + p * own
                wt_ref[pl.ds(p * wide + owner * own, own), :] = turned[start : start + own, :]
        local["dc"].wait()
        local["dr"].wait()
        for ref, i in ((cs_ref, 0), (rs_ref, 1)):
            scale = lax.rsqrt(deg_ref[i].astype(F32))
            for j in range(deg_rows):
                ref[:, pl.ds(j * TILE, TILE)] = scale[j : j + 1, :]
        for i in range(2):
            for ref, line in ((same_ref, 5 * i + 3), (some_ref, 5 * i + 4)):
                flags = table_ref[pl.ds(line, 1), :].astype(F32)
                ref[i] = jnp.broadcast_to(flags, (TILE, TILE)).T
        local["tiles"].wait()
        local["cot"].wait()

    def tiles_times(way, dense, contract, first_tile, tiles):
        @pl.loop(first_tile // GROUP, (first_tile + tiles) // GROUP)
        def step(i):
            products = []
            for j in range(GROUP):
                t = i * GROUP + j
                source = pl.ds(idx_ref[5 * way + 1, t] * TILE, TILE)
                products.append(
                    lax.dot_general(
                        dense(source),
                        tiles_ref[idx_ref[5 * way, t]],
                        contract,
                        preferred_element_type=F32,
                    )
                )
            total = acc_ref[...]
            for j in range(GROUP):
                t = i * GROUP + j
                total = total * same_ref[way, pl.ds(t, 1), :] + products[j]
                seg_ref[t] = total.astype(BF16)
            acc_ref[...] = total

    def clear():
        acc_ref[...] = jnp.zeros_like(acc_ref)

    def collect(way, ref, p):
        @pl.loop(0, blocks)
        def one(b):
            value = seg_ref[idx_ref[5 * way + 2, b]]
            where = pl.ds(pl.multiple_of(b * TILE, TILE), TILE)
            some = some_ref[way, pl.ds(b, 1), :]
            ref[p, :, where] = (value.astype(F32) * some).astype(BF16)

    by_row = (((1,), (1,)), ((), ()))
    by_col = (((1,), (0,)), ((), ()))
    grads = (g0_ref, g1_ref)

    def forward_tiles(p):
        clear()
        tiles_times(0, lambda source: proj_ref[p, :, source], by_row, 0, TILE)
        collect(0, part_ref, p)

    def backward_tiles(p, first_tile, tiles):
        if first_tile == 0:
            clear()
        tiles_times(
            1,
            lambda source: grads[p][:, :, source].reshape(wide, TILE),
            by_col,
            first_tile,
            tiles,
        )
        if first_tile + tiles == TILE:
            collect(1, back_ref, p)

    span = nodes // MID_CHUNKS
    x_rows = own * N_ZH
    x_half = x_rows // 2

    def unit(u):
        p, q = u // MID_CHUNKS, u % MID_CHUNKS
        return p, pl.ds(q * span, span)

    def part(x_of, side, u):
        p, lanes = unit(u)
        start = pl.multiple_of(x_of * x_rows + side * x_half, x_half)
        return part_ref.at[p, pl.ds(start, x_half), lanes]

    def slot(i, u):
        p, lanes = unit(u)
        return in_ref.at[i, p, :, lanes]

    def merged(i, u):
        p, lanes = unit(u)
        return merge_ref.at[i, p, :, lanes]

    def reduce_out(u):
        sent["f0", u] = links.start(part(x_far, 0, u), slot(0, u), x_right)
        sent["f1", u] = links.start(part(x_far, 1, u), slot(1, u), x_left)
        sent["d0", u] = links.start(part(x_up, 1, u), slot(2, u), x_right)
        sent["d1", u] = links.start(part(x_down, 0, u), slot(3, u), x_left)

    def reduce_merge(u):
        sent["f0", u].wait_recv()
        merged(0, u)[...] = add(slot(0, u)[...], part(x_up, 0, u)[...])
        sent["m0", u] = links.start(merged(0, u), slot(4, u), x_right)
        sent["f1", u].wait_recv()
        merged(1, u)[...] = add(slot(1, u)[...], part(x_down, 1, u)[...])
        sent["m1", u] = links.start(merged(1, u), slot(5, u), x_left)

    def reduce_z(u):
        p, lanes = unit(u)
        for name in ("d0", "d1", "m0", "m1"):
            sent[name, u].wait_recv()
        for side, (through, direct) in enumerate(((4, 3), (5, 2))):
            total = slot(through, u)[...].astype(F32) + slot(direct, u)[...].astype(F32)
            total = total + part(x, side, u)[...].astype(F32)
            sum_ref[p, pl.ds(side * x_half, x_half), lanes] = total.astype(BF16)
        for d in range(1, N_ZH):
            rows = pl.ds(pl.multiple_of(((zh + d) % N_ZH) * own, own), own)
            sent["z", d, u] = links.start(
                sum_ref.at[p, rows, lanes], z_ref.at[d - 1, p, :, lanes], zh_group[d - 1]
            )

    def activate(u):
        p, lanes = unit(u)
        value = sum_ref[p, pl.ds(pl.multiple_of(zh * own, own), own), lanes].astype(F32)
        for d in range(1, N_ZH):
            sent["z", d, u].wait_recv()
            value = value + z_ref[d - 1, p, :, lanes].astype(F32)
        scale = rs_ref[:, lanes]
        hidden_in = value * scale
        sigma = 1.0 / (1.0 + jnp.exp(-hidden_in))
        rows = pl.ds(p * own, own)
        out_ref[rows, lanes] = (hidden_in * sigma).astype(BF16)
        slope = sigma * (1.0 + hidden_in * (1.0 - sigma))
        grad = cot_ref[rows, lanes].astype(F32) * slope * scale
        grads[p][h, :, lanes] = grad.astype(BF16)
        mine = grads[p].at[h, :, lanes]
        for d in range(1, N_ZH):
            sent["g", d, u] = links.start(mine, mine, zh_group[d - 1])

    def gather_x(u):
        p, lanes = unit(u)
        for d in range(1, N_ZH):
            sent["g", d, u].wait_recv()
        mine = grads[p].at[pl.ds(x * N_ZH, N_ZH), :, lanes]
        sent["gr", u] = links.start(mine, mine, x_right)
        sent["gl", u] = links.start(mine, mine, x_left)

    def gather_far(u):
        p, lanes = unit(u)
        sent["gr", u].wait_recv()
        near = grads[p].at[pl.ds(x_down * N_ZH, N_ZH // 2), :, lanes]
        sent["hr", u] = links.start(near, near, x_right)
        sent["gl", u].wait_recv()
        near = grads[p].at[pl.ds(x_up * N_ZH + N_ZH // 2, N_ZH // 2), :, lanes]
        sent["hl", u] = links.start(near, near, x_left)

    def gather_end(u):
        sent["hr", u].wait_recv()
        sent["hl", u].wait_recv()

    end_rows = wide // END_CHUNKS
    end_half = end_rows // 2
    side_nodes = nodes // N_CORE
    mine_nodes = nodes // N_ROW
    y_nodes = mine_nodes * N_ZL

    def rows_of_unit(v, start=0, size=end_rows):
        return pl.ds(v * end_rows + start, size)

    def core_out(v):
        p, r = v // END_CHUNKS, v % END_CHUNKS
        there = pl.ds(pl.multiple_of((1 - core) * side_nodes, side_nodes), side_nodes)
        src = back_ref.at[p, pl.ds(r * end_rows, end_rows), there]
        sent["c", v] = links.start(src, core_ref.at[rows_of_unit(v), :], c_peer)

    def y_part(y_of, side, v):
        lanes = pl.ds(pl.multiple_of(y_of * y_nodes, y_nodes), y_nodes)
        return half_ref.at[rows_of_unit(v, side * end_half, end_half), lanes]

    def yslot(i, v):
        return yin_ref.at[i, pl.ds(v * end_half, end_half), :]

    def ymerged(i, v):
        return ymerge_ref.at[i, pl.ds(v * end_half, end_half), :]

    def y_out(v):
        p, r = v // END_CHUNKS, v % END_CHUNKS
        sent["c", v].wait_recv()
        step = min(side_nodes, 512)

        @pl.loop(0, side_nodes // step)
        def one(j):
            here = pl.ds(pl.multiple_of(j * step, step), step)
            there = pl.ds(pl.multiple_of(core * side_nodes + j * step, step), step)
            half_ref[rows_of_unit(v), here] = add(
                back_ref[p, pl.ds(r * end_rows, end_rows), there], core_ref[rows_of_unit(v), here]
            )

        sent["yf0", v] = links.start(y_part(y_far, 0, v), yslot(0, v), y_right)
        sent["yf1", v] = links.start(y_part(y_far, 1, v), yslot(1, v), y_left)
        sent["yd0", v] = links.start(y_part(y_up, 1, v), yslot(2, v), y_right)
        sent["yd1", v] = links.start(y_part(y_down, 0, v), yslot(3, v), y_left)

    def y_merge(v):
        sent["yf0", v].wait_recv()
        ymerged(0, v)[...] = add(yslot(0, v)[...], y_part(y_up, 0, v)[...])
        sent["ym0", v] = links.start(ymerged(0, v), yslot(4, v), y_right)
        sent["yf1", v].wait_recv()
        ymerged(1, v)[...] = add(yslot(1, v)[...], y_part(y_down, 1, v)[...])
        sent["ym1", v] = links.start(ymerged(1, v), yslot(5, v), y_left)

    def z_out(v):
        for name in ("yd0", "yd1", "ym0", "ym1"):
            sent[name, v].wait_recv()
        for side, (through, direct) in enumerate(((4, 3), (5, 2))):
            total = yslot(through, v)[...].astype(F32) + yslot(direct, v)[...].astype(F32)
            total = total + y_part(y, side, v)[...].astype(F32)
            ysum_ref[rows_of_unit(v, side * end_half, end_half), :] = total.astype(BF16)
        there = pl.ds(pl.multiple_of(zp * mine_nodes, mine_nodes), mine_nodes)
        sent["yz", v] = links.start(
            ysum_ref.at[rows_of_unit(v), there], zin_ref.at[rows_of_unit(v), :], z_peer
        )

    place = pl.ds(
        pl.multiple_of(core * side_nodes + (y * N_ZL + zl) * mine_nodes, mine_nodes), mine_nodes
    )

    def scaled(v):
        sent["yz", v].wait_recv()
        here = pl.ds(pl.multiple_of(zl * mine_nodes, mine_nodes), mine_nodes)
        value = ysum_ref[rows_of_unit(v), here].astype(F32) + zin_ref[rows_of_unit(v), :].astype(F32)
        gp_ref[rows_of_unit(v), :] = (value * cs_ref[:, place]).astype(BF16)

    def spread(name, src_of, dst):
        for d in range(1, N_ROW):
            sent[name, d] = links.start(src_of((g + d) % N_ROW), dst, row_group[d - 1])
        return src_of(g)

    def arrived(name):
        for d in range(1, N_ROW):
            sent[name, d].wait_recv()

    def spread_grad(p):
        def piece(owner):
            return gp_ref.at[pl.ds(pl.multiple_of(p * wide + owner * own, own), own), :]

        mine = spread(("gp", p), piece, gpa_ref.at[p, :, place])
        gpa_ref[p, :, place] = mine[...]

    def spread_features():
        gft_ref[...] = lax.dot_general(
            wt_ref[...], gp_ref[...], (((0,), (0,)), ((), ())), preferred_element_type=F32
        ).astype(BF16)

        def piece(owner):
            return gft_ref.at[pl.ds(pl.multiple_of(owner * depth, depth), depth), :]

        mine = spread("gf", piece, gf_ref.at[:, place])
        gf_ref[:, place] = mine[...]

    feats = w_hbm.shape[0]
    weight_total = {}

    def weight_part(p):
        arrived(("gp", p))
        total = jnp.zeros((own, feats), F32)
        step = min(nodes, 512)
        for j in range(nodes // step):
            where = pl.ds(j * step, step)
            total = total + lax.dot_general(
                gpa_ref[p, :, where],
                all_ref[:, :, where].reshape(feats, step),
                (((1,), (1,)), ((), ())),
                preferred_element_type=F32,
            )
        weight_total[p] = total
        share_out("px", p, 0, px_ref, x_group)

    def share_out(name, p, index, buffer, group):
        lw_ref[index, p] = weight_total[p].astype(BF16)
        for i, peer in enumerate(group):
            sent[name, p, i] = links.start(lw_ref.at[index, p], buffer.at[i, p], peer)

    def share_in(name, p, buffer, group):
        for i in range(len(group)):
            sent[name, p, i].wait_recv()
            weight_total[p] = weight_total[p] + buffer[i, p].astype(F32)

    def weight_x(p):
        share_in("px", p, px_ref, x_group)
        share_out("pz", p, 1, pz_ref, zh_group)

    def weight_end(p):
        share_in("pz", p, pz_ref, zh_group)
        gw_ref[pl.ds(p * own, own), :] = weight_total[p]

    ag_stages = (ag_own, ag_z, ag_y, ag_zy, ag_far, project)
    for step in range(AG_CHUNKS + len(ag_stages) - 1):
        for stage, act in enumerate(ag_stages):
            if 0 <= step - stage < AG_CHUNKS:
                act(step - stage)
        if step == 1:
            prepare()

    units = PARTS * MID_CHUNKS
    forward_tiles(0)
    for u in range(MID_CHUNKS):
        reduce_out(u)
    forward_tiles(1)
    mid_stages = (
        reduce_out, reduce_merge, reduce_z, activate, gather_x, gather_far, gather_end,
    )
    steps = units + len(mid_stages) - 1
    ready = MID_CHUNKS - 1 + len(mid_stages) - 1
    pieces = steps - 1 - ready
    for step in range(1, steps):
        for stage, act in enumerate(mid_stages):
            if 0 <= step - stage < units and not (stage == 0 and step < MID_CHUNKS):
                act(step - stage)
        if ready <= step < ready + pieces:
            share = TILE // pieces
            backward_tiles(0, (step - ready) * share, share)

    core_out(0)
    core_out(1)
    y_out(0)
    y_out(1)
    share = TILE // 4
    backward_tiles(1, 0, share)
    y_merge(0)
    backward_tiles(1, share, share)
    y_merge(1)
    backward_tiles(1, 2 * share, share)
    z_out(0)
    backward_tiles(1, 3 * share, share)
    core_out(2)
    core_out(3)
    z_out(1)
    scaled(0)
    y_out(2)
    y_out(3)
    scaled(1)
    spread_grad(0)
    y_merge(2)
    weight_part(0)
    y_merge(3)
    weight_x(0)
    z_out(2)
    weight_end(0)
    z_out(3)
    scaled(2)
    scaled(3)
    spread_grad(1)
    spread_features()
    weight_part(1)
    weight_x(1)
    weight_end(1)
    arrived("gf")
    links.drain()


def shards(features, weight, degrees, tile_values, tile_row, tile_col, tile_count, cotangent):
    nodes, depth = features.shape
    feats, hidden = weight.shape
    wide, own = hidden // PARTS, depth // PARTS
    mine = nodes // N_ROW
    x_half = own * N_ZH // 2
    end_half = wide // 2
    side, y_nodes = nodes // N_CORE, mine * N_ZL
    tiles = tile_values[0, 0]
    vmem = pl.BlockSpec(memory_space=pltpu.VMEM)
    smem = pl.BlockSpec(memory_space=pltpu.SMEM)
    anywhere = pl.BlockSpec(memory_space=pl.ANY)

    def buffer(*shape, dtype=BF16):
        return pltpu.VMEM(shape, dtype)

    table = pl.pallas_call(
        plan_kernel,
        out_shape=jax.ShapeDtypeStruct((16, TILE), I32),
        in_specs=[vmem, vmem, smem],
        out_specs=vmem,
        name="plan",
    )(tile_row[0], tile_col[0], tile_count)
    output, grad_features, grad_weight = pl.pallas_call(
        kernel,
        out_shape=(
            jax.ShapeDtypeStruct((depth, nodes), BF16),
            jax.ShapeDtypeStruct((depth, nodes), BF16),
            jax.ShapeDtypeStruct((depth, feats), F32),
        ),
        in_specs=[anywhere, anywhere, anywhere, anywhere, smem, vmem, anywhere],
        out_specs=(vmem, vmem, vmem),
        scratch_shapes=[
            buffer(N_ROW, depth, nodes),
            buffer(*tiles.shape),
            buffer(feats, hidden),
            buffer(hidden, feats),
            buffer(depth, nodes),
            buffer(2, nodes // TILE, TILE, dtype=I32),
            buffer(1, nodes, dtype=F32),
            buffer(1, nodes, dtype=F32),
            buffer(2, TILE, TILE, dtype=F32),
            buffer(2, TILE, TILE, dtype=F32),
            buffer(PARTS, wide, nodes),
            buffer(TILE, wide, TILE),
            buffer(wide, TILE, dtype=F32),
            buffer(PARTS, wide, nodes),
            buffer(6, PARTS, x_half, nodes),
            buffer(2, PARTS, x_half, nodes),
            buffer(PARTS, 2 * x_half, nodes),
            buffer(N_ZH - 1, PARTS, own, nodes),
            buffer(N_COL, own, nodes),
            buffer(N_COL, own, nodes),
            buffer(PARTS, wide, nodes),
            buffer(hidden, side),
            buffer(hidden, side),
            buffer(6, hidden // 2, y_nodes),
            buffer(2, hidden // 2, y_nodes),
            buffer(hidden, y_nodes),
            buffer(hidden, mine),
            buffer(hidden, mine),
            buffer(feats, mine),
            buffer(PARTS, own, nodes),
            buffer(2, PARTS, own, feats),
            buffer(N_X - 1, PARTS, own, feats),
            buffer(N_ZH - 1, PARTS, own, feats),
            pltpu.SemaphoreType.DMA((8,)),
            pltpu.SemaphoreType.DMA((SENDS,)),
            pltpu.SemaphoreType.DMA((SENDS,)),
        ],
        compiler_params=pltpu.CompilerParams(
            collective_id=0, has_side_effects=True, vmem_limit_bytes=VMEM_BYTES
        ),
        name="layer",
    )(
        features.T,
        weight,
        degrees.reshape(-1, TILE),
        tiles,
        table,
        table,
        cotangent.T,
    )
    return (output.T, grad_features.T, grad_weight.T)


def solution(mesh):
    in_specs = (
        P("col", "row"),
        P(),
        P(),
        P("row", "col", None, None, None),
        P("row", "col", None),
        P("row", "col", None),
        P("row", "col"),
        P("row", "col"),
    )
    out_specs = (P("row", "col"), P("col", "row"), P(None, "row"))
    return jax.shard_map(shards, mesh=mesh, in_specs=in_specs, out_specs=out_specs, check_vma=False)
```

time: 703 us -> 196 us (0.28)
  waiting for transfers between devices: 296 us -> 0 us
  Pallas kernels: 0 us -> 189 us
  other arithmetic: 151 us -> 0 us
  blocking collectives: 82.1 us -> 0 us
  local copies, waits for them, and re-layouts: 83.4 us -> 4.81 us
  matrix products: 72.9 us -> 0 us
  between operations: 14.5 us -> 1.29 us
    pallas_call x0 -> x2, Pallas kernels: none -> 189 us  [the longest x1 187 us: shards(): pl.pallas_call(kernel, out_shape=(jax.ShapeDtypeStruct((depth, nodes), BF...]
    scatter-add x16 -> x0, other arithmetic: 132 us -> none  [accumulate(): jax.ops.segment_sum(product, block_target, num_segments=blocks_out)]
    reduce_scatter x1 -> x0, waiting for transfers between devices: 106 us -> none  [shards(): lax.psum_scatter(partial_value.astype(jnp.bfloat16), 'col', scatter_dimen...]
    all_gather x3 -> x0, waiting for transfers between devices: 105 us -> none  [the longest x1 67.2 us: shards(): grad_rows = lax.all_gather(grad_in, 'col', axis=1, tiled=True)]
    unnamed x6 -> x0, waiting for transfers between devices: 84.2 us -> none
    psum x1 -> x0, blocking collectives: 82.1 us -> none  [shards(): lax.psum(local_weight.astype(jnp.bfloat16), 'col').astype(jnp.float32)]
    dot_general x19 -> x0, matrix products: 72.9 us -> none  [the longest x16 59.1 us: accumulate(): jnp.einsum(form, block_tiles, pieces, preferred_element_type=jnp.float32)]
    gather x16 -> x0, local copies, waits for them, and re-layouts: 45.9 us -> none  [accumulate(): pieces = stacked[block_gather]]
  transfers between devices with their start and end apart: 5 -> 0, of which waited for: 4 -> 0; matrix products, arithmetic and copies ran while one was open for 2% -> 0% of each run, Pallas kernels for 0% -> 0%
where the time goes in v2:
time: 196 us; the launch traced here: 195 us
  Pallas kernels  189 us (96%)
  local copies, waits for them, and re-layouts  4.81 us (2%)
    pallas_call x1, Pallas kernels, shards(): pl.pallas_call(kernel, out_shape=(jax.ShapeDtypeStruct((depth, nodes), BF...  187 us
    unnamed x3, local copies, waits for them, and re-layouts  4.81 us

profile of v2, /device:TPU:0, one launch (start us, length us, event | category | flops | bytes accessed | tf_op | source)
XLA Modules:
  0.0 194.7 jit_solution(4618956929387636506)
XLA Ops:
  1.3 1.5 plan.1.idx_ref.table_ref
  2.8 187.1 %layer.1 = (bf16[32,4096]{1,0:T(8,128)(2,1)}, bf16[32,4096]{1,0:T(8,128)(2,1)}, f32[32,512]{1,0:T(8,128)}) custom-call(bf16[32,4096]{1,0:T(8,128)(2,1)} %bitcast.12, bf16[512,512]{1,0:T(8,128)(2,1)} %w_hbm.1, s32[512,128]{1,0:T(8,128)} %bitcast.13, bf16[128,128,128]{2,1,0:T(8,128)(2,1)} %bitcast.9, s32[16,128]{1,0:T(8,128)} %plan.1.idx_ref.table_ref, ...), custom_call_target="tpu_custom_call" | custom-call | tf_op jit(solution)/shard_map/layer/pallas_call | solution.py:593
  189.9 1.7 copy.15
  191.6 1.7 copy.16
  193.3 1.5 copy.17

commit v3 on v2

--- a/solution.py
+++ b/solution.py
@@ -13,16 +13,17 @@
 AG_CHUNKS = 4
 MID_CHUNKS = 4
 END_CHUNKS = 2
-GROUP = 4
+GROUP = 16
 VMEM_BYTES = 60 * 1024 * 1024
 BF16, F32, I32 = jnp.bfloat16, jnp.float32, jnp.int32
 MESH = pl.DeviceIdType.MESH
 SENDS = (
-    AG_CHUNKS * 17
-    + PARTS * MID_CHUNKS * 16
+    AG_CHUNKS * 20
+    + PARTS * MID_CHUNKS * 20
     + PARTS * END_CHUNKS * 8
     + (PARTS + 1) * (N_ROW - 1)
-    + PARTS * (N_X - 1 + N_ZH - 1)
+    + N_X - 1
+    + N_ZH - 1
 )
 
 
@@ -95,8 +96,8 @@
     out_ref, gf_ref, gw_ref,
     all_ref, tiles_ref, w_ref, wt_ref, cot_ref, deg_ref, cs_ref, rs_ref, same_ref, some_ref,
     proj_ref, seg_ref, acc_ref, part_ref,
-    in_ref, merge_ref, sum_ref, z_ref, g0_ref, g1_ref, back_ref,
-    core_ref, half_ref, yin_ref, ymerge_ref, ysum_ref, zin_ref, gp_ref, gft_ref, gpa_ref,
+    in_ref, merge_ref, sum_ref, z_ref, zmerge_ref, g0_ref, g1_ref, back_ref,
+    core_ref, half_ref, yin_ref, ymerge_ref, ysum_ref, zin_ref, gp_ref, gft_ref, gwt_ref, gwl_ref,
     lw_ref, px_ref, pz_ref, local_sems, send_sems, recv_sems,
 ):
     links = Links(send_sems, recv_sems)
@@ -115,6 +116,8 @@
     z_peer, c_peer = (at(y, zp, core), h), (at(y, zl, 1 - core), h)
     row_group = [((g + d) % N_ROW, h) for d in range(1, N_ROW)]
     x_group = [(g, ((x + d) % N_X) * N_ZH + zh) for d in range(1, N_X)]
+    z_up, z_down, z_far = (zh + 1) % N_ZH, (zh + N_ZH - 1) % N_ZH, (zh + 2) % N_ZH
+    z_right, z_left = (g, x * N_ZH + z_up), (g, x * N_ZH + z_down)
     zh_group = [(g, x * N_ZH + (zh + d) % N_ZH) for d in range(1, N_ZH)]
 
     nodes = x_hbm.shape[1]
@@ -122,6 +125,7 @@
     wide = hidden // PARTS
     depth = x_hbm.shape[0]
     own = depth // PARTS
+    feats = w_hbm.shape[0]
     blocks = nodes // TILE
     deg_rows = nodes // TILE
     sent = {}
@@ -159,31 +163,41 @@
     def ag_z(q):
         sent["z", q].wait_recv()
         owner = at(y, zp, core)
-        for name, device in (("zr", y_right), ("zl", y_left), ("c1", c_peer)):
-            sent[name, q] = forward(owner, q, device)
+        sent["zr", q] = forward(owner, q, y_right, first)
+        sent["zl", q] = forward(owner, q, y_left, first)
+        sent["c1", q] = forward(owner, q, c_peer)
 
     def ag_y(q):
         sent["r", q].wait_recv()
         sent["fr", q] = forward(at(y_down, zl, core), q, y_right, first)
+        sent["rz", q] = forward(at(y_down, zl, core), q, z_peer, second)
         sent["l", q].wait_recv()
         sent["fl", q] = forward(at(y_up, zl, core), q, y_left, second)
+        sent["lz", q] = forward(at(y_up, zl, core), q, z_peer, second)
         sent["c2", q] = forward(at(y_down, zl, core), q, c_peer)
         sent["c3", q] = forward(at(y_up, zl, core), q, c_peer)
 
-    def ag_zy(q):
+    def ag_far(q):
+        sent["fl", q].wait_recv()
+        sent["fz", q] = forward(at(y_far, zl, core), q, z_peer, second)
         sent["zr", q].wait_recv()
-        sent["gr", q] = forward(at(y_down, zp, core), q, y_right, first)
+        lanes = pl.ds(q * ag_span, ag_span // 2)
+        block = all_ref.at[at(y_down, zp, core), first, lanes]
+        sent["gr", q] = links.start(block, block, y_right)
         sent["zl", q].wait_recv()
-        sent["gl", q] = forward(at(y_up, zp, core), q, y_left, second)
-        sent["c4", q] = forward(at(y_down, zp, core), q, c_peer)
-        sent["c5", q] = forward(at(y_up, zp, core), q, c_peer)
-
-    def ag_far(q):
+        lanes = pl.ds(q * ag_span + ag_span // 2, ag_span // 2)
+        block = all_ref.at[at(y_up, zp, core), first, lanes]
+        sent["gl", q] = links.start(block, block, y_left)
         sent["fr", q].wait_recv()
-        sent["fl", q].wait_recv()
-        sent["c6", q] = forward(at(y_far, zl, core), q, c_peer)
-        sent["gr", q].wait_recv()
-        sent["gl", q].wait_recv()
+        sent["c4", q] = forward(at(y_far, zl, core), q, c_peer)
+
+    def ag_last(q):
+        sent["rz", q].wait_recv()
+        sent["c5", q] = forward(at(y_down, zp, core), q, c_peer)
+        sent["lz", q].wait_recv()
+        sent["c6", q] = forward(at(y_up, zp, core), q, c_peer)
+        for name in ("gr", "gl", "fz"):
+            sent[name, q].wait_recv()
         sent["c7", q] = forward(at(y_far, zp, core), q, c_peer)
 
     def project(q):
@@ -321,34 +335,66 @@
             total = slot(through, u)[...].astype(F32) + slot(direct, u)[...].astype(F32)
             total = total + part(x, side, u)[...].astype(F32)
             sum_ref[p, pl.ds(side * x_half, x_half), lanes] = total.astype(BF16)
-        for d in range(1, N_ZH):
-            rows = pl.ds(pl.multiple_of(((zh + d) % N_ZH) * own, own), own)
-            sent["z", d, u] = links.start(
-                sum_ref.at[p, rows, lanes], z_ref.at[d - 1, p, :, lanes], zh_group[d - 1]
-            )
+        sent["zf0", u] = links.start(z_part(z_far, 0, u), z_slot(0, u), z_right)
+        sent["zf1", u] = links.start(z_part(z_far, 1, u), z_slot(1, u), z_left)
+        sent["zd0", u] = links.start(z_part(z_up, 1, u), z_slot(2, u), z_right)
+        sent["zd1", u] = links.start(z_part(z_down, 0, u), z_slot(3, u), z_left)
+
+    def half_lanes(u, side):
+        return pl.ds((u % MID_CHUNKS) * span + side * (span // 2), span // 2)
+
+    def z_part(zh_of, side, u):
+        rows = pl.ds(pl.multiple_of(zh_of * own, own), own)
+        return sum_ref.at[u // MID_CHUNKS, rows, half_lanes(u, side)]
+
+    def z_slot(i, u):
+        return z_ref.at[i, u // MID_CHUNKS, :, pl.ds((u % MID_CHUNKS) * (span // 2), span // 2)]
+
+    def z_merged(i, u):
+        lanes = pl.ds((u % MID_CHUNKS) * (span // 2), span // 2)
+        return zmerge_ref.at[i, u // MID_CHUNKS, :, lanes]
+
+    def merge_z(u):
+        sent["zf0", u].wait_recv()
+        z_merged(0, u)[...] = add(z_slot(0, u)[...], z_part(z_up, 0, u)[...])
+        sent["zm0", u] = links.start(z_merged(0, u), z_slot(4, u), z_right)
+        sent["zf1", u].wait_recv()
+        z_merged(1, u)[...] = add(z_slot(1, u)[...], z_part(z_down, 1, u)[...])
+        sent["zm1", u] = links.start(z_merged(1, u), z_slot(5, u), z_left)
 
     def activate(u):
         p, lanes = unit(u)
-        value = sum_ref[p, pl.ds(pl.multiple_of(zh * own, own), own), lanes].astype(F32)
-        for d in range(1, N_ZH):
-            sent["z", d, u].wait_recv()
-            value = value + z_ref[d - 1, p, :, lanes].astype(F32)
-        scale = rs_ref[:, lanes]
-        hidden_in = value * scale
-        sigma = 1.0 / (1.0 + jnp.exp(-hidden_in))
+        for name in ("zd0", "zd1", "zm0", "zm1"):
+            sent[name, u].wait_recv()
         rows = pl.ds(p * own, own)
-        out_ref[rows, lanes] = (hidden_in * sigma).astype(BF16)
-        slope = sigma * (1.0 + hidden_in * (1.0 - sigma))
-        grad = cot_ref[rows, lanes].astype(F32) * slope * scale
-        grads[p][h, :, lanes] = grad.astype(BF16)
+        for side, (through, direct) in enumerate(((4, 3), (5, 2))):
+            here = half_lanes(u, side)
+            value = z_slot(through, u)[...].astype(F32) + z_slot(direct, u)[...].astype(F32)
+            value = value + z_part(zh, side, u)[...].astype(F32)
+            scale = rs_ref[:, here]
+            hidden_in = value * scale
+            sigma = 1.0 / (1.0 + jnp.exp(-hidden_in))
+            out_ref[rows, here] = (hidden_in * sigma).astype(BF16)
+            slope = sigma * (1.0 + hidden_in * (1.0 - sigma))
+            grad = cot_ref[rows, here].astype(F32) * slope * scale
+            grads[p][h, :, here] = grad.astype(BF16)
         mine = grads[p].at[h, :, lanes]
-        for d in range(1, N_ZH):
-            sent["g", d, u] = links.start(mine, mine, zh_group[d - 1])
+        sent["ar", u] = links.start(mine, mine, z_right)
+        sent["al", u] = links.start(mine, mine, z_left)
+
+    def gather_z(u):
+        p = u // MID_CHUNKS
+        sent["ar", u].wait_recv()
+        near = grads[p].at[x * N_ZH + z_down, :, half_lanes(u, 0)]
+        sent["br", u] = links.start(near, near, z_right)
+        sent["al", u].wait_recv()
+        near = grads[p].at[x * N_ZH + z_up, :, half_lanes(u, 1)]
+        sent["bl", u] = links.start(near, near, z_left)
 
     def gather_x(u):
         p, lanes = unit(u)
-        for d in range(1, N_ZH):
-            sent["g", d, u].wait_recv()
+        sent["br", u].wait_recv()
+        sent["bl", u].wait_recv()
         mine = grads[p].at[pl.ds(x * N_ZH, N_ZH), :, lanes]
         sent["gr", u] = links.start(mine, mine, x_right)
         sent["gl", u] = links.start(mine, mine, x_left)
@@ -448,123 +494,137 @@
         for d in range(1, N_ROW):
             sent[name, d].wait_recv()
 
-    def spread_grad(p):
+    def spread_weight(p):
+        gwt_ref[p] = lax.dot_general(
+            gp_ref[pl.ds(p * wide, wide), :],
+            all_ref[:, :, place].reshape(feats, mine_nodes),
+            (((1,), (1,)), ((), ())),
+            preferred_element_type=F32,
+        ).astype(BF16)
+
         def piece(owner):
-            return gp_ref.at[pl.ds(pl.multiple_of(p * wide + owner * own, own), own), :]
-
-        mine = spread(("gp", p), piece, gpa_ref.at[p, :, place])
-        gpa_ref[p, :, place] = mine[...]
-
-    def spread_features():
+            return gwt_ref.at[p, pl.ds(pl.multiple_of(owner * own, own), own), :]
+
+        spread(("gw", p), piece, gwl_ref.at[p, g])
+
+    def sum_weight(p):
+        arrived(("gw", p))
+        total = gwt_ref[p, pl.ds(pl.multiple_of(g * own, own), own), :].astype(F32)
+        for d in range(1, N_ROW):
+            total = total + gwl_ref[p, (g + d) % N_ROW].astype(F32)
+        gw_ref[pl.ds(p * own, own), :] = total
+
+    def feature_product():
         gft_ref[...] = lax.dot_general(
             wt_ref[...], gp_ref[...], (((0,), (0,)), ((), ())), preferred_element_type=F32
         ).astype(BF16)
 
+    def spread_features():
         def piece(owner):
             return gft_ref.at[pl.ds(pl.multiple_of(owner * depth, depth), depth), :]
 
         mine = spread("gf", piece, gf_ref.at[:, place])
         gf_ref[:, place] = mine[...]
 
-    feats = w_hbm.shape[0]
-    weight_total = {}
-
-    def weight_part(p):
-        arrived(("gp", p))
-        total = jnp.zeros((own, feats), F32)
-        step = min(nodes, 512)
-        for j in range(nodes // step):
-            where = pl.ds(j * step, step)
-            total = total + lax.dot_general(
-                gpa_ref[p, :, where],
-                all_ref[:, :, where].reshape(feats, step),
-                (((1,), (1,)), ((), ())),
-                preferred_element_type=F32,
-            )
-        weight_total[p] = total
-        share_out("px", p, 0, px_ref, x_group)
-
-    def share_out(name, p, index, buffer, group):
-        lw_ref[index, p] = weight_total[p].astype(BF16)
+    def share_out(name, index, buffer, group):
+        lw_ref[index] = gw_ref[...].astype(BF16)
         for i, peer in enumerate(group):
-            sent[name, p, i] = links.start(lw_ref.at[index, p], buffer.at[i, p], peer)
-
-    def share_in(name, p, buffer, group):
+            sent[name, i] = links.start(lw_ref.at[index], buffer.at[i], peer)
+
+    def share_in(name, buffer, group):
+        total = gw_ref[...]
         for i in range(len(group)):
-            sent[name, p, i].wait_recv()
-            weight_total[p] = weight_total[p] + buffer[i, p].astype(F32)
-
-    def weight_x(p):
-        share_in("px", p, px_ref, x_group)
-        share_out("pz", p, 1, pz_ref, zh_group)
-
-    def weight_end(p):
-        share_in("pz", p, pz_ref, zh_group)
-        gw_ref[pl.ds(p * own, own), :] = weight_total[p]
-
-    ag_stages = (ag_own, ag_z, ag_y, ag_zy, ag_far, project)
-    for step in range(AG_CHUNKS + len(ag_stages) - 1):
-        for stage, act in enumerate(ag_stages):
-            if 0 <= step - stage < AG_CHUNKS:
-                act(step - stage)
-        if step == 1:
-            prepare()
+            sent[name, i].wait_recv()
+            total = total + buffer[i].astype(F32)
+        gw_ref[...] = total
+
+    for q in range(AG_CHUNKS):
+        ag_own(q)
+    prepare()
+    for q in range(AG_CHUNKS):
+        ag_z(q)
+        ag_y(q)
+    ag_far(0)
+    ag_far(1)
+    ag_last(0)
+    ag_far(2)
+    ag_last(1)
+    project(0)
+    ag_far(3)
+    ag_last(2)
+    project(1)
+    ag_last(3)
+    project(2)
+    project(3)
 
     units = PARTS * MID_CHUNKS
+    share = TILE // 4
     forward_tiles(0)
-    for u in range(MID_CHUNKS):
-        reduce_out(u)
+    reduce_out(0)
+    reduce_out(1)
     forward_tiles(1)
     mid_stages = (
-        reduce_out, reduce_merge, reduce_z, activate, gather_x, gather_far, gather_end,
+        (0, reduce_merge), (-2, reduce_out), (1, reduce_z), (2, merge_z), (3, activate),
+        (4, gather_z), (5, gather_x), (6, gather_far),
     )
-    steps = units + len(mid_stages) - 1
-    ready = MID_CHUNKS - 1 + len(mid_stages) - 1
-    pieces = steps - 1 - ready
-    for step in range(1, steps):
-        for stage, act in enumerate(mid_stages):
-            if 0 <= step - stage < units and not (stage == 0 and step < MID_CHUNKS):
-                act(step - stage)
-        if ready <= step < ready + pieces:
-            share = TILE // pieces
-            backward_tiles(0, (step - ready) * share, share)
-
-    core_out(0)
-    core_out(1)
-    y_out(0)
-    y_out(1)
-    share = TILE // 4
+    for step in range(units + 6):
+        for lag, act in mid_stages:
+            u = step - lag
+            if 0 <= u < units and not (act is reduce_out and u < 2):
+                act(u)
+        if step == units + 2:
+            for u in range(MID_CHUNKS):
+                gather_end(u)
+            backward_tiles(0, 0, share)
+            backward_tiles(0, share, share)
+        if step == units + 3:
+            backward_tiles(0, 2 * share, share)
+            backward_tiles(0, 3 * share, share)
+            core_out(0)
+            core_out(1)
+        if step == units + 4:
+            y_out(0)
+            y_out(1)
+    y_merge(0)
+    for u in range(MID_CHUNKS, units):
+        gather_end(u)
     backward_tiles(1, 0, share)
-    y_merge(0)
+    y_merge(1)
     backward_tiles(1, share, share)
-    y_merge(1)
+    z_out(0)
     backward_tiles(1, 2 * share, share)
-    z_out(0)
+    z_out(1)
     backward_tiles(1, 3 * share, share)
     core_out(2)
     core_out(3)
-    z_out(1)
     scaled(0)
+    scaled(1)
     y_out(2)
     y_out(3)
-    scaled(1)
-    spread_grad(0)
     y_merge(2)
-    weight_part(0)
     y_merge(3)
-    weight_x(0)
+    spread_weight(0)
     z_out(2)
-    weight_end(0)
     z_out(3)
     scaled(2)
     scaled(3)
-    spread_grad(1)
+    spread_weight(1)
+    sum_weight(0)
+    feature_product()
+    sum_weight(1)
+    share_out("px", 0, px_ref, x_group)
     spread_features()
-    weight_part(1)
-    weight_x(1)
-    weight_end(1)
+    share_in("px", px_ref, x_group)
+    share_out("pz", 1, pz_ref, zh_group)
+    share_in("pz", pz_ref, zh_group)
     arrived("gf")
     links.drain()
+
+
+def write_kernel(*refs):
+    count = len(refs) // 2
+    for i in range(count):
+        refs[count + i][...] = refs[i][...]
 
 
 def shards(features, weight, degrees, tile_values, tile_row, tile_col, tile_count, cotangent):
@@ -590,7 +650,7 @@
         out_specs=vmem,
         name="plan",
     )(tile_row[0], tile_col[0], tile_count)
-    output, grad_features, grad_weight = pl.pallas_call(
+    results = pl.pallas_call(
         kernel,
         out_shape=(
             jax.ShapeDtypeStruct((depth, nodes), BF16),
@@ -617,7 +677,8 @@
             buffer(6, PARTS, x_half, nodes),
             buffer(2, PARTS, x_half, nodes),
             buffer(PARTS, 2 * x_half, nodes),
-            buffer(N_ZH - 1, PARTS, own, nodes),
+            buffer(6, PARTS, own, nodes // 2),
+            buffer(2, PARTS, own, nodes // 2),
             buffer(N_COL, own, nodes),
             buffer(N_COL, own, nodes),
             buffer(PARTS, wide, nodes),
@@ -629,10 +690,11 @@
             buffer(hidden, mine),
             buffer(hidden, mine),
             buffer(feats, mine),
-            buffer(PARTS, own, nodes),
-            buffer(2, PARTS, own, feats),
-            buffer(N_X - 1, PARTS, own, feats),
-            buffer(N_ZH - 1, PARTS, own, feats),
+            buffer(PARTS, wide, feats),
+            buffer(PARTS, N_ROW, own, feats),
+            buffer(2, depth, feats),
+            buffer(N_X - 1, depth, feats),
+            buffer(N_ZH - 1, depth, feats),
             pltpu.SemaphoreType.DMA((8,)),
             pltpu.SemaphoreType.DMA((SENDS,)),
             pltpu.SemaphoreType.DMA((SENDS,)),
@@ -650,6 +712,13 @@
         table,
         cotangent.T,
     )
+    output, grad_features, grad_weight = pl.pallas_call(
+        write_kernel,
+        out_shape=tuple(jax.ShapeDtypeStruct(r.shape, r.dtype) for r in results),
+        in_specs=[vmem] * len(results),
+        out_specs=(vmem,) * len(results),
+        name="write",
+    )(*results)
     return (output.T, grad_features.T, grad_weight.T)
 
 

time: 196 us -> 159 us (0.81)
  Pallas kernels: 189 us -> 157 us
  local copies, waits for them, and re-layouts: 4.81 us -> 0 us
    pallas_call x1, Pallas kernels: 187 us -> 153 us  [shards(): pl.pallas_call(kernel, out_shape=(jax.ShapeDtypeStruct((depth, nodes), BF...]
    unnamed x3 -> x0, local copies, waits for them, and re-layouts: 4.81 us -> none
where the time goes in v3:
time: 159 us; the launch traced here: 158 us
  Pallas kernels  157 us (99%)
    pallas_call x1, Pallas kernels, shards(): pl.pallas_call(kernel, out_shape=(jax.ShapeDtypeStruct((depth, nodes), BF...  153 us

profile of v3, /device:TPU:0, one launch (start us, length us, event | category | flops | bytes accessed | tf_op | source)
XLA Modules:
  0.0 158.0 jit_solution(5671558574598920796)
XLA Ops:
  1.3 1.5 plan.1.idx_ref.table_ref
  2.8 153.4 %layer.1 = (bf16[32,4096]{1,0:T(8,128)(2,1)}, bf16[32,4096]{1,0:T(8,128)(2,1)}, f32[32,512]{1,0:T(8,128)}) custom-call(bf16[32,4096]{1,0:T(8,128)(2,1)} %bitcast.10, bf16[512,512]{1,0:T(8,128)(2,1)} %w_hbm.1, s32[512,128]{1,0:T(8,128)} %bitcast.11, bf16[128,128,128]{2,1,0:T(8,128)(2,1)} %bitcast.9, s32[16,128]{1,0:T(8,128)} %plan.1.idx_ref.table_ref, ...), custom_call_target="tpu_custom_call" | custom-call | tf_op jit(solution)/shard_map/layer/pallas_call | solution.py:653
  156.2 1.9 %write.1 = (bf16[32,4096]{1,0:T(8,128)(2,1)}, bf16[32,4096]{1,0:T(8,128)(2,1)}, f32[32,512]{1,0:T(8,128)}) custom-call(bf16[32,4096]{1,0:T(8,128)(2,1)} %get-tuple-element.9.refs_0_, bf16[32,4096]{1,0:T(8,128)(2,1)} %get-tuple-element.10.refs_1_, f32[32,512]{1,0:T(8,128)} %get-tuple-element.11.refs_2_), custom_call_target="tpu_custom_call" | custom-call | tf_op jit(solution)/shard_map/write/pallas_call | solution.py:715

commit v4 on v3

--- a/solution.py
+++ b/solution.py
@@ -13,6 +13,7 @@
 AG_CHUNKS = 4
 MID_CHUNKS = 4
 END_CHUNKS = 2
+Z_FIRST = (4,)
 GROUP = 16
 VMEM_BYTES = 60 * 1024 * 1024
 BF16, F32, I32 = jnp.bfloat16, jnp.float32, jnp.int32
@@ -22,8 +23,7 @@
     + PARTS * MID_CHUNKS * 20
     + PARTS * END_CHUNKS * 8
     + (PARTS + 1) * (N_ROW - 1)
-    + N_X - 1
-    + N_ZH - 1
+    + PARTS * (N_X - 1 + N_ZH - 1)
 )
 
 
@@ -205,17 +205,16 @@
             sent["c%d" % i, q].wait_recv()
         if q == 0:
             local["x"].wait()
-        step = min(ag_span, 256)
+        step = min(ag_span, 512)
 
         @pl.loop(0, ag_span // step)
         def one(j):
             where = pl.ds(pl.multiple_of(q * ag_span + j * step, step), step)
             block = all_ref[:, :, where].reshape(-1, step)
+            value = jnp.dot(wt_ref[...], block, preferred_element_type=F32)
+            value = (value * cs_ref[:, where]).astype(BF16)
             for p in range(PARTS):
-                value = jnp.dot(
-                    wt_ref[pl.ds(p * wide, wide), :], block, preferred_element_type=F32
-                )
-                proj_ref[p, :, where] = (value * cs_ref[:, where]).astype(BF16)
+                proj_ref[p, :, where] = value[p * wide : (p + 1) * wide, :]
 
     def prepare():
         local["w"].wait()
@@ -268,7 +267,11 @@
             value = seg_ref[idx_ref[5 * way + 2, b]]
             where = pl.ds(pl.multiple_of(b * TILE, TILE), TILE)
             some = some_ref[way, pl.ds(b, 1), :]
-            ref[p, :, where] = (value.astype(F32) * some).astype(BF16)
+            value = (value.astype(F32) * some).astype(BF16)
+            if len(ref.shape) == 3:
+                ref[p, :, where] = value
+            else:
+                ref[p, :, :, :, where] = value.reshape(N_X, N_ZH, own, TILE)
 
     by_row = (((1,), (1,)), ((), ()))
     by_col = (((1,), (0,)), ((), ()))
@@ -284,7 +287,7 @@
             clear()
         tiles_times(
             1,
-            lambda source: grads[p][:, :, source].reshape(wide, TILE),
+            lambda source: grads[p][:, :, :, source].reshape(wide, TILE),
             by_col,
             first_tile,
             tiles,
@@ -293,120 +296,142 @@
             collect(1, back_ref, p)
 
     span = nodes // MID_CHUNKS
-    x_rows = own * N_ZH
-    x_half = x_rows // 2
+    pair = N_X // 2
+    ring = {
+        "x": (x, x_up, x_down, x_far, x_right, x_left),
+        "z": (zh, z_up, z_down, z_far, z_right, z_left),
+    }
+
+    def axes(u):
+        return ("z", "x") if u in Z_FIRST else ("x", "z")
 
     def unit(u):
         p, q = u // MID_CHUNKS, u % MID_CHUNKS
         return p, pl.ds(q * span, span)
 
-    def part(x_of, side, u):
+    def half_lanes(u, side):
+        return pl.ds((u % MID_CHUNKS) * span + side * (span // 2), span // 2)
+
+    def grid(ref, axis, along, across, lanes):
+        if axis == "x":
+            return ref.at[along, across, :, lanes]
+        return ref.at[across, along, :, lanes]
+
+    def part(coord, side, u):
         p, lanes = unit(u)
-        start = pl.multiple_of(x_of * x_rows + side * x_half, x_half)
-        return part_ref.at[p, pl.ds(start, x_half), lanes]
+        return grid(part_ref.at[p], axes(u)[0], coord, pl.ds(side * pair, pair), lanes)
 
     def slot(i, u):
         p, lanes = unit(u)
-        return in_ref.at[i, p, :, lanes]
+        return in_ref.at[i, p, :, :, lanes]
 
     def merged(i, u):
         p, lanes = unit(u)
-        return merge_ref.at[i, p, :, lanes]
+        return merge_ref.at[i, p, :, :, lanes]
 
     def reduce_out(u):
-        sent["f0", u] = links.start(part(x_far, 0, u), slot(0, u), x_right)
-        sent["f1", u] = links.start(part(x_far, 1, u), slot(1, u), x_left)
-        sent["d0", u] = links.start(part(x_up, 1, u), slot(2, u), x_right)
-        sent["d1", u] = links.start(part(x_down, 0, u), slot(3, u), x_left)
+        me, up, down, far, right, left = ring[axes(u)[0]]
+        sent["f0", u] = links.start(part(far, 0, u), slot(0, u), right)
+        sent["f1", u] = links.start(part(far, 1, u), slot(1, u), left)
+        sent["d0", u] = links.start(part(up, 1, u), slot(2, u), right)
+        sent["d1", u] = links.start(part(down, 0, u), slot(3, u), left)
 
     def reduce_merge(u):
+        me, up, down, far, right, left = ring[axes(u)[0]]
         sent["f0", u].wait_recv()
-        merged(0, u)[...] = add(slot(0, u)[...], part(x_up, 0, u)[...])
-        sent["m0", u] = links.start(merged(0, u), slot(4, u), x_right)
+        merged(0, u)[...] = add(slot(0, u)[...], part(up, 0, u)[...])
+        sent["m0", u] = links.start(merged(0, u), slot(4, u), right)
         sent["f1", u].wait_recv()
-        merged(1, u)[...] = add(slot(1, u)[...], part(x_down, 1, u)[...])
-        sent["m1", u] = links.start(merged(1, u), slot(5, u), x_left)
-
-    def reduce_z(u):
+        merged(1, u)[...] = add(slot(1, u)[...], part(down, 1, u)[...])
+        sent["m1", u] = links.start(merged(1, u), slot(5, u), left)
+
+    def second_part(coord, side, u):
+        return sum_ref.at[u // MID_CHUNKS, coord, :, half_lanes(u, side)]
+
+    def second_slot(i, u):
+        return z_ref.at[i, u // MID_CHUNKS, :, pl.ds((u % MID_CHUNKS) * (span // 2), span // 2)]
+
+    def second_merged(i, u):
+        lanes = pl.ds((u % MID_CHUNKS) * (span // 2), span // 2)
+        return zmerge_ref.at[i, u // MID_CHUNKS, :, lanes]
+
+    def reduce_second(u):
         p, lanes = unit(u)
+        me = ring[axes(u)[0]][0]
         for name in ("d0", "d1", "m0", "m1"):
             sent[name, u].wait_recv()
         for side, (through, direct) in enumerate(((4, 3), (5, 2))):
             total = slot(through, u)[...].astype(F32) + slot(direct, u)[...].astype(F32)
-            total = total + part(x, side, u)[...].astype(F32)
-            sum_ref[p, pl.ds(side * x_half, x_half), lanes] = total.astype(BF16)
-        sent["zf0", u] = links.start(z_part(z_far, 0, u), z_slot(0, u), z_right)
-        sent["zf1", u] = links.start(z_part(z_far, 1, u), z_slot(1, u), z_left)
-        sent["zd0", u] = links.start(z_part(z_up, 1, u), z_slot(2, u), z_right)
-        sent["zd1", u] = links.start(z_part(z_down, 0, u), z_slot(3, u), z_left)
-
-    def half_lanes(u, side):
-        return pl.ds((u % MID_CHUNKS) * span + side * (span // 2), span // 2)
-
-    def z_part(zh_of, side, u):
-        rows = pl.ds(pl.multiple_of(zh_of * own, own), own)
-        return sum_ref.at[u // MID_CHUNKS, rows, half_lanes(u, side)]
-
-    def z_slot(i, u):
-        return z_ref.at[i, u // MID_CHUNKS, :, pl.ds((u % MID_CHUNKS) * (span // 2), span // 2)]
-
-    def z_merged(i, u):
-        lanes = pl.ds((u % MID_CHUNKS) * (span // 2), span // 2)
-        return zmerge_ref.at[i, u // MID_CHUNKS, :, lanes]
-
-    def merge_z(u):
+            total = total + part(me, side, u)[...].astype(F32)
+            sum_ref[p, pl.ds(side * pair, pair), :, lanes] = total.astype(BF16)
+        me, up, down, far, right, left = ring[axes(u)[1]]
+        sent["zf0", u] = links.start(second_part(far, 0, u), second_slot(0, u), right)
+        sent["zf1", u] = links.start(second_part(far, 1, u), second_slot(1, u), left)
+        sent["zd0", u] = links.start(second_part(up, 1, u), second_slot(2, u), right)
+        sent["zd1", u] = links.start(second_part(down, 0, u), second_slot(3, u), left)
+
+    def merge_second(u):
+        me, up, down, far, right, left = ring[axes(u)[1]]
         sent["zf0", u].wait_recv()
-        z_merged(0, u)[...] = add(z_slot(0, u)[...], z_part(z_up, 0, u)[...])
-        sent["zm0", u] = links.start(z_merged(0, u), z_slot(4, u), z_right)
+        second_merged(0, u)[...] = add(second_slot(0, u)[...], second_part(up, 0, u)[...])
+        sent["zm0", u] = links.start(second_merged(0, u), second_slot(4, u), right)
         sent["zf1", u].wait_recv()
-        z_merged(1, u)[...] = add(z_slot(1, u)[...], z_part(z_down, 1, u)[...])
-        sent["zm1", u] = links.start(z_merged(1, u), z_slot(5, u), z_left)
+        second_merged(1, u)[...] = add(second_slot(1, u)[...], second_part(down, 1, u)[...])
+        sent["zm1", u] = links.start(second_merged(1, u), second_slot(5, u), left)
 
     def activate(u):
         p, lanes = unit(u)
+        me, up, down, far, right, left = ring[axes(u)[1]]
         for name in ("zd0", "zd1", "zm0", "zm1"):
             sent[name, u].wait_recv()
         rows = pl.ds(p * own, own)
         for side, (through, direct) in enumerate(((4, 3), (5, 2))):
             here = half_lanes(u, side)
-            value = z_slot(through, u)[...].astype(F32) + z_slot(direct, u)[...].astype(F32)
-            value = value + z_part(zh, side, u)[...].astype(F32)
+            value = second_slot(through, u)[...].astype(F32)
+            value = value + second_slot(direct, u)[...].astype(F32)
+            value = value + second_part(me, side, u)[...].astype(F32)
             scale = rs_ref[:, here]
             hidden_in = value * scale
             sigma = 1.0 / (1.0 + jnp.exp(-hidden_in))
             out_ref[rows, here] = (hidden_in * sigma).astype(BF16)
             slope = sigma * (1.0 + hidden_in * (1.0 - sigma))
             grad = cot_ref[rows, here].astype(F32) * slope * scale
-            grads[p][h, :, here] = grad.astype(BF16)
-        mine = grads[p].at[h, :, lanes]
-        sent["ar", u] = links.start(mine, mine, z_right)
-        sent["al", u] = links.start(mine, mine, z_left)
-
-    def gather_z(u):
-        p = u // MID_CHUNKS
+            grads[p][x, zh, :, here] = grad.astype(BF16)
+        mine = grads[p].at[x, zh, :, lanes]
+        sent["ar", u] = links.start(mine, mine, right)
+        sent["al", u] = links.start(mine, mine, left)
+
+    def gather_second(u):
+        first_axis, axis = axes(u)
+        me, up, down, far, right, left = ring[axis]
+        across, ref = ring[first_axis][0], grads[u // MID_CHUNKS]
         sent["ar", u].wait_recv()
-        near = grads[p].at[x * N_ZH + z_down, :, half_lanes(u, 0)]
-        sent["br", u] = links.start(near, near, z_right)
+        near = grid(ref, axis, down, across, half_lanes(u, 0))
+        sent["br", u] = links.start(near, near, right)
         sent["al", u].wait_recv()
-        near = grads[p].at[x * N_ZH + z_up, :, half_lanes(u, 1)]
-        sent["bl", u] = links.start(near, near, z_left)
-
-    def gather_x(u):
+        near = grid(ref, axis, up, across, half_lanes(u, 1))
+        sent["bl", u] = links.start(near, near, left)
+
+    def gather_first(u):
         p, lanes = unit(u)
+        axis = axes(u)[0]
+        me, up, down, far, right, left = ring[axis]
         sent["br", u].wait_recv()
         sent["bl", u].wait_recv()
-        mine = grads[p].at[pl.ds(x * N_ZH, N_ZH), :, lanes]
-        sent["gr", u] = links.start(mine, mine, x_right)
-        sent["gl", u] = links.start(mine, mine, x_left)
+        mine = grid(grads[p], axis, me, slice(None), lanes)
+        sent["gr", u] = links.start(mine, mine, right)
+        sent["gl", u] = links.start(mine, mine, left)
 
     def gather_far(u):
         p, lanes = unit(u)
+        axis = axes(u)[0]
+        me, up, down, far, right, left = ring[axis]
         sent["gr", u].wait_recv()
-        near = grads[p].at[pl.ds(x_down * N_ZH, N_ZH // 2), :, lanes]
-        sent["hr", u] = links.start(near, near, x_right)
+        near = grid(grads[p], axis, down, pl.ds(0, pair), lanes)
+        sent["hr", u] = links.start(near, near, right)
         sent["gl", u].wait_recv()
-        near = grads[p].at[pl.ds(x_up * N_ZH + N_ZH // 2, N_ZH // 2), :, lanes]
-        sent["hl", u] = links.start(near, near, x_left)
+        near = grid(grads[p], axis, up, pl.ds(pair, pair), lanes)
+        sent["hl", u] = links.start(near, near, left)
 
     def gather_end(u):
         sent["hr", u].wait_recv()
@@ -526,17 +551,18 @@
         mine = spread("gf", piece, gf_ref.at[:, place])
         gf_ref[:, place] = mine[...]
 
-    def share_out(name, index, buffer, group):
-        lw_ref[index] = gw_ref[...].astype(BF16)
+    def share_out(name, p, buffer, group):
+        sums = lw_ref.at[0 if name == "px" else 1, p]
+        sums[...] = gw_ref[pl.ds(p * own, own), :].astype(BF16)
         for i, peer in enumerate(group):
-            sent[name, i] = links.start(lw_ref.at[index], buffer.at[i], peer)
-
-    def share_in(name, buffer, group):
-        total = gw_ref[...]
+            sent[name, p, i] = links.start(sums, buffer.at[i, p], peer)
+
+    def share_in(name, p, buffer, group):
+        total = gw_ref[pl.ds(p * own, own), :]
         for i in range(len(group)):
-            sent[name, i].wait_recv()
-            total = total + buffer[i].astype(F32)
-        gw_ref[...] = total
+            sent[name, p, i].wait_recv()
+            total = total + buffer[i, p].astype(F32)
+        gw_ref[pl.ds(p * own, own), :] = total
 
     for q in range(AG_CHUNKS):
         ag_own(q)
@@ -548,9 +574,9 @@
     ag_far(1)
     ag_last(0)
     ag_far(2)
+    ag_far(3)
     ag_last(1)
     project(0)
-    ag_far(3)
     ag_last(2)
     project(1)
     ag_last(3)
@@ -563,60 +589,70 @@
     reduce_out(0)
     reduce_out(1)
     forward_tiles(1)
-    mid_stages = (
-        (0, reduce_merge), (-2, reduce_out), (1, reduce_z), (2, merge_z), (3, activate),
-        (4, gather_z), (5, gather_x), (6, gather_far),
+    x_lags = (
+        (0, reduce_merge), (-2, reduce_out), (1, reduce_second), (2, merge_second),
+        (3, activate), (4, gather_second), (5, gather_first), (6, gather_far),
     )
-    for step in range(units + 6):
-        for lag, act in mid_stages:
-            u = step - lag
-            if 0 <= u < units and not (act is reduce_out and u < 2):
-                act(u)
-        if step == units + 2:
+    z_lags = (
+        (0, reduce_out), (2, reduce_merge), (3, reduce_second), (4, merge_second),
+        (6, activate), (7, gather_second), (8, gather_first), (10, gather_far),
+    )
+    x_first = [u for u in range(units) if u not in Z_FIRST]
+    steps = len(x_first) + 6
+    for step in range(steps):
+        for lag, act in x_lags:
+            if max(0, -lag) <= step - lag < len(x_first):
+                act(x_first[step - lag])
+        for lag, act in z_lags:
+            for u in Z_FIRST:
+                if step == lag:
+                    act(u)
+        if step == steps - 4:
             for u in range(MID_CHUNKS):
                 gather_end(u)
-            backward_tiles(0, 0, share)
-            backward_tiles(0, share, share)
-        if step == units + 3:
-            backward_tiles(0, 2 * share, share)
-            backward_tiles(0, 3 * share, share)
+            backward_tiles(0, 0, 2 * share)
+        if step == steps - 3:
+            backward_tiles(0, 2 * share, 2 * share)
             core_out(0)
             core_out(1)
-        if step == units + 4:
+        if step == steps - 2:
             y_out(0)
             y_out(1)
-    y_merge(0)
     for u in range(MID_CHUNKS, units):
         gather_end(u)
     backward_tiles(1, 0, share)
+    y_merge(0)
+    backward_tiles(1, share, share)
     y_merge(1)
-    backward_tiles(1, share, share)
-    z_out(0)
-    backward_tiles(1, 2 * share, share)
-    z_out(1)
-    backward_tiles(1, 3 * share, share)
+    backward_tiles(1, 2 * share, 2 * share)
     core_out(2)
     core_out(3)
+    z_out(0)
+    z_out(1)
+    y_out(2)
+    y_out(3)
     scaled(0)
     scaled(1)
-    y_out(2)
-    y_out(3)
     y_merge(2)
     y_merge(3)
     spread_weight(0)
     z_out(2)
     z_out(3)
+    sum_weight(0)
+    share_out("px", 0, px_ref, x_group)
     scaled(2)
     scaled(3)
     spread_weight(1)
-    sum_weight(0)
+    share_in("px", 0, px_ref, x_group)
+    share_out("pz", 0, pz_ref, zh_group)
     feature_product()
     sum_weight(1)
-    share_out("px", 0, px_ref, x_group)
+    share_out("px", 1, px_ref, x_group)
     spread_features()
-    share_in("px", px_ref, x_group)
+    share_in("pz", 0, pz_ref, zh_group)
+    share_in("px", 1, px_ref, x_group)
     share_out("pz", 1, pz_ref, zh_group)
-    share_in("pz", pz_ref, zh_group)
+    share_in("pz", 1, pz_ref, zh_group)
     arrived("gf")
     links.drain()
 
@@ -632,8 +668,6 @@
     feats, hidden = weight.shape
     wide, own = hidden // PARTS, depth // PARTS
     mine = nodes // N_ROW
-    x_half = own * N_ZH // 2
-    end_half = wide // 2
     side, y_nodes = nodes // N_CORE, mine * N_ZL
     tiles = tile_values[0, 0]
     vmem = pl.BlockSpec(memory_space=pltpu.VMEM)
@@ -673,14 +707,14 @@
             buffer(PARTS, wide, nodes),
             buffer(TILE, wide, TILE),
             buffer(wide, TILE, dtype=F32),
-            buffer(PARTS, wide, nodes),
-            buffer(6, PARTS, x_half, nodes),
-            buffer(2, PARTS, x_half, nodes),
-            buffer(PARTS, 2 * x_half, nodes),
+            buffer(PARTS, N_X, N_ZH, own, nodes),
+            buffer(6, PARTS, N_X // 2, own, nodes),
+            buffer(2, PARTS, N_X // 2, own, nodes),
+            buffer(PARTS, N_X, own, nodes),
             buffer(6, PARTS, own, nodes // 2),
             buffer(2, PARTS, own, nodes // 2),
-            buffer(N_COL, own, nodes),
-            buffer(N_COL, own, nodes),
+            buffer(N_X, N_ZH, own, nodes),
+            buffer(N_X, N_ZH, own, nodes),
             buffer(PARTS, wide, nodes),
             buffer(hidden, side),
             buffer(hidden, side),
@@ -692,9 +726,9 @@
             buffer(feats, mine),
             buffer(PARTS, wide, feats),
             buffer(PARTS, N_ROW, own, feats),
-            buffer(2, depth, feats),
-            buffer(N_X - 1, depth, feats),
-            buffer(N_ZH - 1, depth, feats),
+            buffer(2, PARTS, own, feats),
+            buffer(N_X - 1, PARTS, own, feats),
+            buffer(N_ZH - 1, PARTS, own, feats),
             pltpu.SemaphoreType.DMA((8,)),
             pltpu.SemaphoreType.DMA((SENDS,)),
             pltpu.SemaphoreType.DMA((SENDS,)),

time: 159 us -> 154 us (0.969)
  Pallas kernels: 157 us -> 150 us
    pallas_call x1, Pallas kernels: 153 us -> 147 us  [shards(): pl.pallas_call(kernel, out_shape=(jax.ShapeDtypeStruct((depth, nodes), BF...]
where the time goes in v4:
time: 154 us; the launch traced here: 152 us
  Pallas kernels  150 us (97%)
    pallas_call x1, Pallas kernels, shards(): pl.pallas_call(kernel, out_shape=(jax.ShapeDtypeStruct((depth, nodes), BF...  147 us

profile of v4, /device:TPU:0, one launch (start us, length us, event | category | flops | bytes accessed | tf_op | source)
XLA Modules:
  0.0 151.7 jit_solution(12640296554522582055)
XLA Ops:
  1.3 1.5 %plan.1.idx_ref.table_ref = s32[16,128]{1,0:T(8,128)} custom-call(s32[1,128]{1,0:T(1,128)} %bitcast.13, s32[1,128]{1,0:T(1,128)} %bitcast.14, s32[1,1]{1,0:T(1,128)S(6)} %copy.11.count_ref), custom_call_target="tpu_custom_call" | custom-call | tf_op jit(solution)/shard_map/plan/pallas_call | solution.py:680
  2.8 147.0 %layer.1 = (bf16[32,4096]{1,0:T(8,128)(2,1)}, bf16[32,4096]{1,0:T(8,128)(2,1)}, f32[32,512]{1,0:T(8,128)}) custom-call(bf16[32,4096]{1,0:T(8,128)(2,1)} %bitcast.10, bf16[512,512]{1,0:T(8,128)(2,1)} %w_hbm.1, s32[512,128]{1,0:T(8,128)} %bitcast.11, bf16[128,128,128]{2,1,0:T(8,128)(2,1)} %bitcast.9, s32[16,128]{1,0:T(8,128)} %plan.1.idx_ref.table_ref, ...), custom_call_target="tpu_custom_call" | custom-call | tf_op jit(solution)/shard_map/layer/pallas_call | solution.py:687
  149.8 1.9 %write.1 = (bf16[32,4096]{1,0:T(8,128)(2,1)}, bf16[32,4096]{1,0:T(8,128)(2,1)}, f32[32,512]{1,0:T(8,128)}) custom-call(bf16[32,4096]{1,0:T(8,128)(2,1)} %get-tuple-element.9.refs_0_, bf16[32,4096]{1,0:T(8,128)(2,1)} %get-tuple-element.10.refs_1_, f32[32,512]{1,0:T(8,128)} %get-tuple-element.11.refs_2_), custom_call_target="tpu_custom_call" | custom-call | tf_op jit(solution)/shard_map/write/pallas_call | solution.py:749

commit v5 on v4

--- a/solution.py
+++ b/solution.py
@@ -14,39 +14,46 @@
 MID_CHUNKS = 4
 END_CHUNKS = 2
 Z_FIRST = (4,)
-GROUP = 16
+GROUP = 32
 VMEM_BYTES = 60 * 1024 * 1024
 BF16, F32, I32 = jnp.bfloat16, jnp.float32, jnp.int32
 MESH = pl.DeviceIdType.MESH
-SENDS = (
-    AG_CHUNKS * 20
-    + PARTS * MID_CHUNKS * 20
-    + PARTS * END_CHUNKS * 8
-    + (PARTS + 1) * (N_ROW - 1)
-    + PARTS * (N_X - 1 + N_ZH - 1)
-)
+SENDS = 64
+RECEIVES = AG_CHUNKS * 13 + PARTS * MID_CHUNKS * 8 + PARTS * END_CHUNKS * 4 + PARTS * 3 + 1
 
 
 class Links:
     def __init__(self, send_sems, recv_sems):
-        self.send_sems, self.recv_sems, self.used, self.open = send_sems, recv_sems, 0, []
-
-    def start(self, src, dst, device):
+        self.send_sems, self.recv_sems, self.copies, self.groups, self.used = (
+            send_sems, recv_sems, [], {}, 0
+        )
+
+    def start(self, src, dst, device, group=None):
+        count = len(self.copies)
+        if count >= SENDS:
+            self.copies[count - SENDS].wait_send()
+        place = self.groups.get(group)
+        if place is None:
+            place, self.used = self.used, self.used + 1
+            if group is not None:
+                self.groups[group] = place
         copy = pltpu.make_async_remote_copy(
             src_ref=src,
             dst_ref=dst,
-            send_sem=self.send_sems.at[self.used],
-            recv_sem=self.recv_sems.at[self.used],
+            send_sem=self.send_sems.at[count % SENDS],
+            recv_sem=self.recv_sems.at[place],
             device_id=device,
             device_id_type=MESH,
         )
-        self.used += 1
         copy.start()
-        self.open.append(copy)
+        self.copies.append(copy)
         return copy
 
+    def wait(self, group, like):
+        pltpu.make_async_copy(like, like, self.recv_sems.at[self.groups[group]]).wait()
+
     def drain(self):
-        for copy in self.open:
+        for copy in self.copies[-SENDS:]:
             copy.wait_send()
 
 
@@ -151,21 +158,22 @@
     def ag_lanes(q):
         return pl.ds(q * ag_span, ag_span)
 
-    def forward(owner, q, device, rows=slice(None)):
+    def forward(owner, q, device, rows=slice(None), group=None):
         block = all_ref.at[owner, rows, ag_lanes(q)]
-        return links.start(block, block, device)
+        return links.start(block, block, device, group)
 
     def ag_own(q):
         src = x_hbm.at[:, ag_lanes(q)]
-        for name, device in (("z", z_peer), ("r", y_right), ("l", y_left), ("c0", c_peer)):
+        for name, device in (("z", z_peer), ("r", y_right), ("l", y_left)):
             sent[name, q] = links.start(src, all_ref.at[g, :, ag_lanes(q)], device)
+        links.start(src, all_ref.at[g, :, ag_lanes(q)], c_peer, ("core", q))
 
     def ag_z(q):
         sent["z", q].wait_recv()
         owner = at(y, zp, core)
         sent["zr", q] = forward(owner, q, y_right, first)
         sent["zl", q] = forward(owner, q, y_left, first)
-        sent["c1", q] = forward(owner, q, c_peer)
+        forward(owner, q, c_peer, group=("core", q))
 
     def ag_y(q):
         sent["r", q].wait_recv()
@@ -174,8 +182,8 @@
         sent["l", q].wait_recv()
         sent["fl", q] = forward(at(y_up, zl, core), q, y_left, second)
         sent["lz", q] = forward(at(y_up, zl, core), q, z_peer, second)
-        sent["c2", q] = forward(at(y_down, zl, core), q, c_peer)
-        sent["c3", q] = forward(at(y_up, zl, core), q, c_peer)
+        forward(at(y_down, zl, core), q, c_peer, group=("core", q))
+        forward(at(y_up, zl, core), q, c_peer, group=("core", q))
 
     def ag_far(q):
         sent["fl", q].wait_recv()
@@ -189,20 +197,19 @@
         block = all_ref.at[at(y_up, zp, core), first, lanes]
         sent["gl", q] = links.start(block, block, y_left)
         sent["fr", q].wait_recv()
-        sent["c4", q] = forward(at(y_far, zl, core), q, c_peer)
+        forward(at(y_far, zl, core), q, c_peer, group=("core", q))
 
     def ag_last(q):
         sent["rz", q].wait_recv()
-        sent["c5", q] = forward(at(y_down, zp, core), q, c_peer)
+        forward(at(y_down, zp, core), q, c_peer, group=("core", q))
         sent["lz", q].wait_recv()
-        sent["c6", q] = forward(at(y_up, zp, core), q, c_peer)
+        forward(at(y_up, zp, core), q, c_peer, group=("core", q))
         for name in ("gr", "gl", "fz"):
             sent[name, q].wait_recv()
-        sent["c7", q] = forward(at(y_far, zp, core), q, c_peer)
+        forward(at(y_far, zp, core), q, c_peer, group=("core", q))
 
     def project(q):
-        for i in range(8):
-            sent["c%d" % i, q].wait_recv()
+        links.wait(("core", q), all_ref.at[pl.ds(0, N_Y * N_ZL), :, ag_lanes(q)])
         if q == 0:
             local["x"].wait()
         step = min(ag_span, 512)
@@ -331,22 +338,26 @@
 
     def reduce_out(u):
         me, up, down, far, right, left = ring[axes(u)[0]]
-        sent["f0", u] = links.start(part(far, 0, u), slot(0, u), right)
-        sent["f1", u] = links.start(part(far, 1, u), slot(1, u), left)
-        sent["d0", u] = links.start(part(up, 1, u), slot(2, u), right)
-        sent["d1", u] = links.start(part(down, 0, u), slot(3, u), left)
+        links.start(part(far, 0, u), slot(0, u), right, ("f", u))
+        links.start(part(far, 1, u), slot(1, u), left, ("f", u))
+        links.start(part(up, 1, u), slot(2, u), right, ("d", u))
+        links.start(part(down, 0, u), slot(3, u), left, ("d", u))
 
     def reduce_merge(u):
         me, up, down, far, right, left = ring[axes(u)[0]]
-        sent["f0", u].wait_recv()
+        p, lanes = unit(u)
+        links.wait(("f", u), in_ref.at[pl.ds(0, 2), p, :, :, lanes])
         merged(0, u)[...] = add(slot(0, u)[...], part(up, 0, u)[...])
-        sent["m0", u] = links.start(merged(0, u), slot(4, u), right)
-        sent["f1", u].wait_recv()
+        links.start(merged(0, u), slot(4, u), right, ("d", u))
         merged(1, u)[...] = add(slot(1, u)[...], part(down, 1, u)[...])
-        sent["m1", u] = links.start(merged(1, u), slot(5, u), left)
+        links.start(merged(1, u), slot(5, u), left, ("d", u))
 
     def second_part(coord, side, u):
         return sum_ref.at[u // MID_CHUNKS, coord, :, half_lanes(u, side)]
+
+    def second_slots(i, count, u):
+        lanes = pl.ds((u % MID_CHUNKS) * (span // 2), span // 2)
+        return z_ref.at[pl.ds(i, count), u // MID_CHUNKS, :, lanes]
 
     def second_slot(i, u):
         return z_ref.at[i, u // MID_CHUNKS, :, pl.ds((u % MID_CHUNKS) * (span // 2), span // 2)]
@@ -358,32 +369,29 @@
     def reduce_second(u):
         p, lanes = unit(u)
         me = ring[axes(u)[0]][0]
-        for name in ("d0", "d1", "m0", "m1"):
-            sent[name, u].wait_recv()
+        links.wait(("d", u), in_ref.at[pl.ds(0, 4), p, :, :, lanes])
         for side, (through, direct) in enumerate(((4, 3), (5, 2))):
             total = slot(through, u)[...].astype(F32) + slot(direct, u)[...].astype(F32)
             total = total + part(me, side, u)[...].astype(F32)
             sum_ref[p, pl.ds(side * pair, pair), :, lanes] = total.astype(BF16)
         me, up, down, far, right, left = ring[axes(u)[1]]
-        sent["zf0", u] = links.start(second_part(far, 0, u), second_slot(0, u), right)
-        sent["zf1", u] = links.start(second_part(far, 1, u), second_slot(1, u), left)
-        sent["zd0", u] = links.start(second_part(up, 1, u), second_slot(2, u), right)
-        sent["zd1", u] = links.start(second_part(down, 0, u), second_slot(3, u), left)
+        links.start(second_part(far, 0, u), second_slot(0, u), right, ("zf", u))
+        links.start(second_part(far, 1, u), second_slot(1, u), left, ("zf", u))
+        links.start(second_part(up, 1, u), second_slot(2, u), right, ("zd", u))
+        links.start(second_part(down, 0, u), second_slot(3, u), left, ("zd", u))
 
     def merge_second(u):
         me, up, down, far, right, left = ring[axes(u)[1]]
-        sent["zf0", u].wait_recv()
+        links.wait(("zf", u), second_slots(0, 2, u))
         second_merged(0, u)[...] = add(second_slot(0, u)[...], second_part(up, 0, u)[...])
-        sent["zm0", u] = links.start(second_merged(0, u), second_slot(4, u), right)
-        sent["zf1", u].wait_recv()
+        links.start(second_merged(0, u), second_slot(4, u), right, ("zd", u))
         second_merged(1, u)[...] = add(second_slot(1, u)[...], second_part(down, 1, u)[...])
-        sent["zm1", u] = links.start(second_merged(1, u), second_slot(5, u), left)
+        links.start(second_merged(1, u), second_slot(5, u), left, ("zd", u))
 
     def activate(u):
         p, lanes = unit(u)
         me, up, down, far, right, left = ring[axes(u)[1]]
-        for name in ("zd0", "zd1", "zm0", "zm1"):
-            sent[name, u].wait_recv()
+        links.wait(("zd", u), second_slots(0, 4, u))
         rows = pl.ds(p * own, own)
         for side, (through, direct) in enumerate(((4, 3), (5, 2))):
             here = half_lanes(u, side)
@@ -398,50 +406,47 @@
             grad = cot_ref[rows, here].astype(F32) * slope * scale
             grads[p][x, zh, :, here] = grad.astype(BF16)
         mine = grads[p].at[x, zh, :, lanes]
-        sent["ar", u] = links.start(mine, mine, right)
-        sent["al", u] = links.start(mine, mine, left)
+        links.start(mine, mine, right, ("a", u))
+        links.start(mine, mine, left, ("a", u))
 
     def gather_second(u):
         first_axis, axis = axes(u)
         me, up, down, far, right, left = ring[axis]
         across, ref = ring[first_axis][0], grads[u // MID_CHUNKS]
-        sent["ar", u].wait_recv()
+        lanes = unit(u)[1]
+        links.wait(("a", u), ref.at[0, pl.ds(0, 2), :, lanes])
         near = grid(ref, axis, down, across, half_lanes(u, 0))
-        sent["br", u] = links.start(near, near, right)
-        sent["al", u].wait_recv()
+        links.start(near, near, right, ("b", u))
         near = grid(ref, axis, up, across, half_lanes(u, 1))
-        sent["bl", u] = links.start(near, near, left)
+        links.start(near, near, left, ("b", u))
 
     def gather_first(u):
         p, lanes = unit(u)
         axis = axes(u)[0]
         me, up, down, far, right, left = ring[axis]
-        sent["br", u].wait_recv()
-        sent["bl", u].wait_recv()
+        links.wait(("b", u), grads[p].at[0, 0, :, lanes])
         mine = grid(grads[p], axis, me, slice(None), lanes)
-        sent["gr", u] = links.start(mine, mine, right)
-        sent["gl", u] = links.start(mine, mine, left)
+        links.start(mine, mine, right, ("g", u))
+        links.start(mine, mine, left, ("g", u))
 
     def gather_far(u):
         p, lanes = unit(u)
         axis = axes(u)[0]
         me, up, down, far, right, left = ring[axis]
-        sent["gr", u].wait_recv()
+        links.wait(("g", u), grads[p].at[pl.ds(0, 2), :, :, lanes])
         near = grid(grads[p], axis, down, pl.ds(0, pair), lanes)
-        sent["hr", u] = links.start(near, near, right)
-        sent["gl", u].wait_recv()
+        links.start(near, near, right, ("h", u))
         near = grid(grads[p], axis, up, pl.ds(pair, pair), lanes)
-        sent["hl", u] = links.start(near, near, left)
+        links.start(near, near, left, ("h", u))
 
     def gather_end(u):
-        sent["hr", u].wait_recv()
-        sent["hl", u].wait_recv()
+        p, lanes = unit(u)
+        links.wait(("h", u), grads[p].at[0, :, :, lanes])
 
     end_rows = wide // END_CHUNKS
     end_half = end_rows // 2
     side_nodes = nodes // N_CORE
     mine_nodes = nodes // N_ROW
-    y_nodes = mine_nodes * N_ZL
 
     def rows_of_unit(v, start=0, size=end_rows):
         return pl.ds(v * end_rows + start, size)
@@ -452,52 +457,83 @@
         src = back_ref.at[p, pl.ds(r * end_rows, end_rows), there]
         sent["c", v] = links.start(src, core_ref.at[rows_of_unit(v), :], c_peer)
 
-    def y_part(y_of, side, v):
-        lanes = pl.ds(pl.multiple_of(y_of * y_nodes, y_nodes), y_nodes)
-        return half_ref.at[rows_of_unit(v, side * end_half, end_half), lanes]
-
-    def yslot(i, v):
-        return yin_ref.at[i, pl.ds(v * end_half, end_half), :]
-
-    def ymerged(i, v):
-        return ymerge_ref.at[i, pl.ds(v * end_half, end_half), :]
-
-    def y_out(v):
+    def core_sum(v):
         p, r = v // END_CHUNKS, v % END_CHUNKS
         sent["c", v].wait_recv()
-        step = min(side_nodes, 512)
-
-        @pl.loop(0, side_nodes // step)
-        def one(j):
-            here = pl.ds(pl.multiple_of(j * step, step), step)
-            there = pl.ds(pl.multiple_of(core * side_nodes + j * step, step), step)
-            half_ref[rows_of_unit(v), here] = add(
+        for j in range(N_Y * N_ZL):
+            here = pl.ds(j * mine_nodes, mine_nodes)
+            there = pl.ds(
+                pl.multiple_of(core * side_nodes + j * mine_nodes, mine_nodes), mine_nodes
+            )
+            half_ref[j // N_ZL, j % N_ZL, rows_of_unit(v), :] = add(
                 back_ref[p, pl.ds(r * end_rows, end_rows), there], core_ref[rows_of_unit(v), here]
             )
 
-        sent["yf0", v] = links.start(y_part(y_far, 0, v), yslot(0, v), y_right)
-        sent["yf1", v] = links.start(y_part(y_far, 1, v), yslot(1, v), y_left)
-        sent["yd0", v] = links.start(y_part(y_up, 1, v), yslot(2, v), y_right)
-        sent["yd1", v] = links.start(y_part(y_down, 0, v), yslot(3, v), y_left)
+    def y_part(y_of, side, v):
+        rows = rows_of_unit(v, side * end_half, end_half)
+        if v % 2:
+            return ysum_ref.at[pl.ds(y_of, 1), rows, :]
+        return half_ref.at[y_of, :, rows, :]
+
+    def y_buffer(ref, i, v):
+        rows = pl.ds(v * end_half, end_half)
+        return ref.at[i, pl.ds(0, 1) if v % 2 else slice(None), rows, :]
+
+    def yslots(count, v):
+        return y_buffer(yin_ref, pl.ds(0, count), v)
+
+    def yslot(i, v):
+        return y_buffer(yin_ref, i, v)
+
+    def ymerged(i, v):
+        return y_buffer(ymerge_ref, i, v)
+
+    def y_send(v):
+        links.start(y_part(y_far, 0, v), yslot(0, v), y_right, ("yf", v))
+        links.start(y_part(y_far, 1, v), yslot(1, v), y_left, ("yf", v))
+        links.start(y_part(y_up, 1, v), yslot(2, v), y_right, ("yd", v))
+        links.start(y_part(y_down, 0, v), yslot(3, v), y_left, ("yd", v))
+
+    def y_out(v):
+        core_sum(v)
+        y_send(v)
+
+    def z_first(v):
+        core_sum(v)
+        sent["yz", v] = links.start(
+            half_ref.at[:, zp, rows_of_unit(v), :], zin_ref.at[:, rows_of_unit(v), :], z_peer
+        )
+
+    def z_then_y(v):
+        sent["yz", v].wait_recv()
+        for j in range(N_Y):
+            ysum_ref[j, rows_of_unit(v), :] = add(
+                half_ref[j, zl, rows_of_unit(v), :], zin_ref[j, rows_of_unit(v), :]
+            )
+        y_send(v)
 
     def y_merge(v):
-        sent["yf0", v].wait_recv()
+        links.wait(("yf", v), yslots(2, v))
         ymerged(0, v)[...] = add(yslot(0, v)[...], y_part(y_up, 0, v)[...])
-        sent["ym0", v] = links.start(ymerged(0, v), yslot(4, v), y_right)
-        sent["yf1", v].wait_recv()
+        links.start(ymerged(0, v), yslot(4, v), y_right, ("yd", v))
         ymerged(1, v)[...] = add(yslot(1, v)[...], y_part(y_down, 1, v)[...])
-        sent["ym1", v] = links.start(ymerged(1, v), yslot(5, v), y_left)
+        links.start(ymerged(1, v), yslot(5, v), y_left, ("yd", v))
+
+    def y_total(v, side):
+        through, direct = ((4, 3), (5, 2))[side]
+        total = yslot(through, v)[...].astype(F32) + yslot(direct, v)[...].astype(F32)
+        return total + y_part(y, side, v)[...].astype(F32)
+
+    def y_arrived(v):
+        links.wait(("yd", v), yslots(4, v))
 
     def z_out(v):
-        for name in ("yd0", "yd1", "ym0", "ym1"):
-            sent[name, v].wait_recv()
-        for side, (through, direct) in enumerate(((4, 3), (5, 2))):
-            total = yslot(through, v)[...].astype(F32) + yslot(direct, v)[...].astype(F32)
-            total = total + y_part(y, side, v)[...].astype(F32)
-            ysum_ref[rows_of_unit(v, side * end_half, end_half), :] = total.astype(BF16)
-        there = pl.ds(pl.multiple_of(zp * mine_nodes, mine_nodes), mine_nodes)
+        y_arrived(v)
+        for side in range(2):
+            rows = rows_of_unit(v, side * end_half, end_half)
+            ysum_ref[pl.ds(0, N_ZL), rows, :] = y_total(v, side).astype(BF16)
         sent["yz", v] = links.start(
-            ysum_ref.at[rows_of_unit(v), there], zin_ref.at[rows_of_unit(v), :], z_peer
+            ysum_ref.at[zp, rows_of_unit(v), :], zin_ref.at[0, rows_of_unit(v), :], z_peer
         )
 
     place = pl.ds(
@@ -505,19 +541,21 @@
     )
 
     def scaled(v):
+        if v % 2:
+            y_arrived(v)
+            for side in range(2):
+                rows = rows_of_unit(v, side * end_half, end_half)
+                gp_ref[rows, :] = (y_total(v, side)[0] * cs_ref[:, place]).astype(BF16)
+            return
         sent["yz", v].wait_recv()
-        here = pl.ds(pl.multiple_of(zl * mine_nodes, mine_nodes), mine_nodes)
-        value = ysum_ref[rows_of_unit(v), here].astype(F32) + zin_ref[rows_of_unit(v), :].astype(F32)
-        gp_ref[rows_of_unit(v), :] = (value * cs_ref[:, place]).astype(BF16)
+        rows = rows_of_unit(v)
+        value = ysum_ref[zl, rows, :].astype(F32) + zin_ref[0, rows, :].astype(F32)
+        gp_ref[rows, :] = (value * cs_ref[:, place]).astype(BF16)
 
     def spread(name, src_of, dst):
         for d in range(1, N_ROW):
-            sent[name, d] = links.start(src_of((g + d) % N_ROW), dst, row_group[d - 1])
+            links.start(src_of((g + d) % N_ROW), dst, row_group[d - 1], name)
         return src_of(g)
-
-    def arrived(name):
-        for d in range(1, N_ROW):
-            sent[name, d].wait_recv()
 
     def spread_weight(p):
         gwt_ref[p] = lax.dot_general(
@@ -533,7 +571,7 @@
         spread(("gw", p), piece, gwl_ref.at[p, g])
 
     def sum_weight(p):
-        arrived(("gw", p))
+        links.wait(("gw", p), gwl_ref.at[p, pl.ds(0, N_ROW - 1)])
         total = gwt_ref[p, pl.ds(pl.multiple_of(g * own, own), own), :].astype(F32)
         for d in range(1, N_ROW):
             total = total + gwl_ref[p, (g + d) % N_ROW].astype(F32)
@@ -555,28 +593,35 @@
         sums = lw_ref.at[0 if name == "px" else 1, p]
         sums[...] = gw_ref[pl.ds(p * own, own), :].astype(BF16)
         for i, peer in enumerate(group):
-            sent[name, p, i] = links.start(sums, buffer.at[i, p], peer)
+            links.start(sums, buffer.at[i, p], peer, (name, p))
 
     def share_in(name, p, buffer, group):
         total = gw_ref[pl.ds(p * own, own), :]
+        links.wait((name, p), buffer.at[:, p])
         for i in range(len(group)):
-            sent[name, p, i].wait_recv()
             total = total + buffer[i, p].astype(F32)
         gw_ref[pl.ds(p * own, own), :] = total
 
-    for q in range(AG_CHUNKS):
-        ag_own(q)
+    ag_own(0)
+    ag_own(1)
+    ag_own(2)
     prepare()
-    for q in range(AG_CHUNKS):
-        ag_z(q)
-        ag_y(q)
+    ag_z(0)
+    ag_y(0)
+    ag_own(3)
+    ag_z(1)
+    ag_y(1)
     ag_far(0)
+    ag_z(2)
+    ag_y(2)
     ag_far(1)
     ag_last(0)
+    ag_z(3)
+    ag_y(3)
     ag_far(2)
-    ag_far(3)
     ag_last(1)
     project(0)
+    ag_far(3)
     ag_last(2)
     project(1)
     ag_last(3)
@@ -595,7 +640,7 @@
     )
     z_lags = (
         (0, reduce_out), (2, reduce_merge), (3, reduce_second), (4, merge_second),
-        (6, activate), (7, gather_second), (8, gather_first), (10, gather_far),
+        (6, activate), (7, gather_second), (9, gather_first), (11, gather_far),
     )
     x_first = [u for u in range(units) if u not in Z_FIRST]
     steps = len(x_first) + 6
@@ -607,53 +652,51 @@
             for u in Z_FIRST:
                 if step == lag:
                     act(u)
-        if step == steps - 4:
+        if step == steps - 3:
             for u in range(MID_CHUNKS):
                 gather_end(u)
-            backward_tiles(0, 0, 2 * share)
-        if step == steps - 3:
-            backward_tiles(0, 2 * share, 2 * share)
+            backward_tiles(0, 0, TILE)
+            core_out(1)
             core_out(0)
-            core_out(1)
         if step == steps - 2:
+            z_first(1)
             y_out(0)
-            y_out(1)
     for u in range(MID_CHUNKS, units):
         gather_end(u)
     backward_tiles(1, 0, share)
     y_merge(0)
     backward_tiles(1, share, share)
+    z_then_y(1)
+    backward_tiles(1, 2 * share, 2 * share)
+    core_out(3)
+    core_out(2)
     y_merge(1)
-    backward_tiles(1, 2 * share, 2 * share)
-    core_out(2)
-    core_out(3)
     z_out(0)
-    z_out(1)
+    z_first(3)
     y_out(2)
-    y_out(3)
+    scaled(1)
     scaled(0)
-    scaled(1)
+    spread_weight(0)
     y_merge(2)
+    z_then_y(3)
+    z_out(2)
     y_merge(3)
-    spread_weight(0)
-    z_out(2)
-    z_out(3)
-    sum_weight(0)
-    share_out("px", 0, px_ref, x_group)
     scaled(2)
     scaled(3)
     spread_weight(1)
+    sum_weight(0)
+    share_out("px", 0, px_ref, x_group)
+    feature_product()
     share_in("px", 0, px_ref, x_group)
     share_out("pz", 0, pz_ref, zh_group)
-    feature_product()
     sum_weight(1)
     share_out("px", 1, px_ref, x_group)
     spread_features()
-    share_in("pz", 0, pz_ref, zh_group)
     share_in("px", 1, px_ref, x_group)
     share_out("pz", 1, pz_ref, zh_group)
+    share_in("pz", 0, pz_ref, zh_group)
     share_in("pz", 1, pz_ref, zh_group)
-    arrived("gf")
+    links.wait("gf", gft_ref.at[pl.ds(0, (N_ROW - 1) * depth), :])
     links.drain()
 
 
@@ -668,7 +711,7 @@
     feats, hidden = weight.shape
     wide, own = hidden // PARTS, depth // PARTS
     mine = nodes // N_ROW
-    side, y_nodes = nodes // N_CORE, mine * N_ZL
+    side = nodes // N_CORE
     tiles = tile_values[0, 0]
     vmem = pl.BlockSpec(memory_space=pltpu.VMEM)
     smem = pl.BlockSpec(memory_space=pltpu.SMEM)
@@ -717,11 +760,11 @@
             buffer(N_X, N_ZH, own, nodes),
             buffer(PARTS, wide, nodes),
             buffer(hidden, side),
-            buffer(hidden, side),
-            buffer(6, hidden // 2, y_nodes),
-            buffer(2, hidden // 2, y_nodes),
-            buffer(hidden, y_nodes),
-            buffer(hidden, mine),
+            buffer(N_Y, N_ZL, hidden, mine),
+            buffer(6, N_ZL, hidden // 2, mine),
+            buffer(2, N_ZL, hidden // 2, mine),
+            buffer(N_Y, hidden, mine),
+            buffer(N_Y, hidden, mine),
             buffer(hidden, mine),
             buffer(feats, mine),
             buffer(PARTS, wide, feats),
@@ -731,7 +774,7 @@
             buffer(N_ZH - 1, PARTS, own, feats),
             pltpu.SemaphoreType.DMA((8,)),
             pltpu.SemaphoreType.DMA((SENDS,)),
-            pltpu.SemaphoreType.DMA((SENDS,)),
+            pltpu.SemaphoreType.DMA((RECEIVES,)),
         ],
         compiler_params=pltpu.CompilerParams(
             collective_id=0, has_side_effects=True, vmem_limit_bytes=VMEM_BYTES

time: 154 us -> 146 us (0.948)
  Pallas kernels: 150 us -> 143 us
    pallas_call x1, Pallas kernels: 147 us -> 139 us  [shards(): pl.pallas_call(kernel, out_shape=(jax.ShapeDtypeStruct((depth, nodes), BF...]
where the time goes in v5:
time: 146 us; the launch traced here: 144 us
  Pallas kernels  143 us (98%)
    pallas_call x1, Pallas kernels, shards(): pl.pallas_call(kernel, out_shape=(jax.ShapeDtypeStruct((depth, nodes), BF...  139 us

profile of v5, /device:TPU:0, one launch (start us, length us, event | category | flops | bytes accessed | tf_op | source)
XLA Modules:
  0.0 144.1 jit_solution(12459076820651204113)
XLA Ops:
  1.3 1.5 %plan.1.idx_ref.table_ref = s32[16,128]{1,0:T(8,128)} custom-call(s32[1,128]{1,0:T(1,128)} %bitcast.13, s32[1,128]{1,0:T(1,128)} %bitcast.14, s32[1,1]{1,0:T(1,128)S(6)} %copy.11.count_ref), custom_call_target="tpu_custom_call" | custom-call | tf_op jit(solution)/shard_map/plan/pallas_call | solution.py:723
  2.8 139.4 %layer.1 = (bf16[32,4096]{1,0:T(8,128)(2,1)}, bf16[32,4096]{1,0:T(8,128)(2,1)}, f32[32,512]{1,0:T(8,128)}) custom-call(bf16[32,4096]{1,0:T(8,128)(2,1)} %bitcast.10, bf16[512,512]{1,0:T(8,128)(2,1)} %w_hbm.1, s32[512,128]{1,0:T(8,128)} %bitcast.11, bf16[128,128,128]{2,1,0:T(8,128)(2,1)} %bitcast.9, s32[16,128]{1,0:T(8,128)} %plan.1.idx_ref.table_ref, ...), custom_call_target="tpu_custom_call" | custom-call | tf_op jit(solution)/shard_map/layer/pallas_call | solution.py:730
  142.3 1.9 %write.1 = (bf16[32,4096]{1,0:T(8,128)(2,1)}, bf16[32,4096]{1,0:T(8,128)(2,1)}, f32[32,512]{1,0:T(8,128)}) custom-call(bf16[32,4096]{1,0:T(8,128)(2,1)} %get-tuple-element.9.refs_0_, bf16[32,4096]{1,0:T(8,128)(2,1)} %get-tuple-element.10.refs_1_, f32[32,512]{1,0:T(8,128)} %get-tuple-element.11.refs_2_), custom_call_target="tpu_custom_call" | custom-call | tf_op jit(solution)/shard_map/write/pallas_call | solution.py:792

commit v6 on v5

--- a/solution.py
+++ b/solution.py
@@ -18,7 +18,7 @@
 VMEM_BYTES = 60 * 1024 * 1024
 BF16, F32, I32 = jnp.bfloat16, jnp.float32, jnp.int32
 MESH = pl.DeviceIdType.MESH
-SENDS = 64
+SENDS = 40
 RECEIVES = AG_CHUNKS * 13 + PARTS * MID_CHUNKS * 8 + PARTS * END_CHUNKS * 4 + PARTS * 3 + 1
 
 
@@ -74,11 +74,11 @@
     j = lax.broadcasted_iota(I32, shape, 1)
     across = jnp.broadcast_to(key, shape)
     down = across.T
-    before = (down < across) | ((down == across) & (i < j))
-    rank = jnp.broadcast_to(jnp.sum(before.astype(I32), axis=0, keepdims=True), shape).T
+    before = (down < across).astype(I32) + (down == across).astype(I32) * (i < j).astype(I32)
+    rank = jnp.broadcast_to(jnp.sum(before, axis=0, keepdims=True), shape).T
 
     def total(where, value):
-        return jnp.sum(jnp.where(where, value, 0), axis=0, keepdims=True)
+        return jnp.sum(where.astype(I32) * value, axis=0, keepdims=True)
 
     order = total(rank == j, i)
     source = total(rank == j, jnp.broadcast_to(gather, shape).T)
@@ -88,20 +88,10 @@
     return [order, source, last, same, some]
 
 
-def plan_kernel(rows_ref, cols_ref, count_ref, table_ref):
-    live = lax.broadcasted_iota(I32, (1, TILE), 1) < count_ref[0, 0]
-    rows_of, cols_of = rows_ref[...], cols_ref[...]
-    lines = sorted_by(jnp.where(live, rows_of, TILE), cols_of)
-    lines += sorted_by(jnp.where(live, cols_of, TILE), rows_of)
-    table_ref[...] = jnp.zeros_like(table_ref)
-    for i, line in enumerate(lines):
-        table_ref[pl.ds(i, 1), :] = line
-
-
 def kernel(
-    x_hbm, w_hbm, deg_hbm, tiles_hbm, idx_ref, table_ref, cot_hbm,
+    x_hbm, w_hbm, deg_hbm, tiles_hbm, rows_ref, cols_ref, count_ref, cot_hbm,
     out_ref, gf_ref, gw_ref,
-    all_ref, tiles_ref, w_ref, wt_ref, cot_ref, deg_ref, cs_ref, rs_ref, same_ref, some_ref,
+    all_ref, tiles_ref, w_ref, wt_ref, cot_ref, deg_ref, cs_ref, rs_ref, table_ref, idx_ref, same_ref, some_ref,
     proj_ref, seg_ref, acc_ref, part_ref,
     in_ref, merge_ref, sum_ref, z_ref, zmerge_ref, g0_ref, g1_ref, back_ref,
     core_ref, half_ref, yin_ref, ymerge_ref, ysum_ref, zin_ref, gp_ref, gft_ref, gwt_ref, gwl_ref,
@@ -236,10 +226,22 @@
             scale = lax.rsqrt(deg_ref[i].astype(F32))
             for j in range(deg_rows):
                 ref[:, pl.ds(j * TILE, TILE)] = scale[j : j + 1, :]
-        for i in range(2):
-            for ref, line in ((same_ref, 5 * i + 3), (some_ref, 5 * i + 4)):
-                flags = table_ref[pl.ds(line, 1), :].astype(F32)
-                ref[i] = jnp.broadcast_to(flags, (TILE, TILE)).T
+        live = lax.broadcasted_iota(I32, (1, TILE), 1) < jnp.broadcast_to(count_ref[...], (1, TILE))
+        live = live.astype(I32)
+        rows_of, cols_of = rows_ref[...], cols_ref[...]
+        dead = (1 - live) * TILE
+        ways = (
+            sorted_by(live * rows_of + dead, cols_of),
+            sorted_by(live * cols_of + dead, rows_of),
+        )
+        table_ref[...] = jnp.zeros_like(table_ref)
+        for way, lines in enumerate(ways):
+            for i, line in enumerate(lines[:3]):
+                table_ref[pl.ds(3 * way + i, 1), :] = line
+            for ref, line in zip((same_ref, some_ref), lines[3:]):
+                ref[way] = jnp.broadcast_to(line.astype(F32), (TILE, TILE)).T
+        local["idx"] = pltpu.make_async_copy(table_ref, idx_ref, local_sems.at[len(loads)])
+        local["idx"].start()
         local["tiles"].wait()
         local["cot"].wait()
 
@@ -249,11 +251,11 @@
             products = []
             for j in range(GROUP):
                 t = i * GROUP + j
-                source = pl.ds(idx_ref[5 * way + 1, t] * TILE, TILE)
+                source = pl.ds(idx_ref[3 * way + 1, t] * TILE, TILE)
                 products.append(
                     lax.dot_general(
                         dense(source),
-                        tiles_ref[idx_ref[5 * way, t]],
+                        tiles_ref[idx_ref[3 * way, t]],
                         contract,
                         preferred_element_type=F32,
                     )
@@ -271,7 +273,7 @@
     def collect(way, ref, p):
         @pl.loop(0, blocks)
         def one(b):
-            value = seg_ref[idx_ref[5 * way + 2, b]]
+            value = seg_ref[idx_ref[3 * way + 2, b]]
             where = pl.ds(pl.multiple_of(b * TILE, TILE), TILE)
             some = some_ref[way, pl.ds(b, 1), :]
             value = (value.astype(F32) * some).astype(BF16)
@@ -630,6 +632,7 @@
 
     units = PARTS * MID_CHUNKS
     share = TILE // 4
+    local["idx"].wait()
     forward_tiles(0)
     reduce_out(0)
     reduce_out(1)
@@ -714,19 +717,11 @@
     side = nodes // N_CORE
     tiles = tile_values[0, 0]
     vmem = pl.BlockSpec(memory_space=pltpu.VMEM)
-    smem = pl.BlockSpec(memory_space=pltpu.SMEM)
     anywhere = pl.BlockSpec(memory_space=pl.ANY)
 
     def buffer(*shape, dtype=BF16):
         return pltpu.VMEM(shape, dtype)
 
-    table = pl.pallas_call(
-        plan_kernel,
-        out_shape=jax.ShapeDtypeStruct((16, TILE), I32),
-        in_specs=[vmem, vmem, smem],
-        out_specs=vmem,
-        name="plan",
-    )(tile_row[0], tile_col[0], tile_count)
     results = pl.pallas_call(
         kernel,
         out_shape=(
@@ -734,7 +729,7 @@
             jax.ShapeDtypeStruct((depth, nodes), BF16),
             jax.ShapeDtypeStruct((depth, feats), F32),
         ),
-        in_specs=[anywhere, anywhere, anywhere, anywhere, smem, vmem, anywhere],
+        in_specs=[anywhere, anywhere, anywhere, anywhere, vmem, vmem, vmem, anywhere],
         out_specs=(vmem, vmem, vmem),
         scratch_shapes=[
             buffer(N_ROW, depth, nodes),
@@ -745,6 +740,8 @@
             buffer(2, nodes // TILE, TILE, dtype=I32),
             buffer(1, nodes, dtype=F32),
             buffer(1, nodes, dtype=F32),
+            buffer(8, TILE, dtype=I32),
+            pltpu.SMEM((8, TILE), I32),
             buffer(2, TILE, TILE, dtype=F32),
             buffer(2, TILE, TILE, dtype=F32),
             buffer(PARTS, wide, nodes),
@@ -772,7 +769,7 @@
             buffer(2, PARTS, own, feats),
             buffer(N_X - 1, PARTS, own, feats),
             buffer(N_ZH - 1, PARTS, own, feats),
-            pltpu.SemaphoreType.DMA((8,)),
+            pltpu.SemaphoreType.DMA((7,)),
             pltpu.SemaphoreType.DMA((SENDS,)),
             pltpu.SemaphoreType.DMA((RECEIVES,)),
         ],
@@ -785,8 +782,9 @@
         weight,
         degrees.reshape(-1, TILE),
         tiles,
-        table,
-        table,
+        tile_row[0],
+        tile_col[0],
+        tile_count,
         cotangent.T,
     )
     output, grad_features, grad_weight = pl.pallas_call(

time: 146 us -> 144 us (0.986)
  Pallas kernels: 143 us -> 141 us
    pallas_call x1 -> x0, Pallas kernels: 1.54 us -> none  [shards(): pl.pallas_call(plan_kernel, out_shape=jax.ShapeDtypeStruct((16, TILE), I3...]
where the time goes in v6:
time: 144 us; the launch traced here: 142 us
  Pallas kernels  141 us (98%)
    pallas_call x1, Pallas kernels, shards(): pl.pallas_call(kernel, out_shape=(jax.ShapeDtypeStruct((depth, nodes), BF...  139 us

profile of v6, /device:TPU:0, one launch (start us, length us, event | category | flops | bytes accessed | tf_op | source)
XLA Modules:
  0.0 141.8 jit_solution(5863216693517001205)
XLA Ops:
  1.3 138.7 %layer.1 = (bf16[32,4096]{1,0:T(8,128)(2,1)}, bf16[32,4096]{1,0:T(8,128)(2,1)}, f32[32,512]{1,0:T(8,128)}) custom-call(bf16[32,4096]{1,0:T(8,128)(2,1)} %bitcast.10, bf16[512,512]{1,0:T(8,128)(2,1)} %w_hbm.1, s32[512,128]{1,0:T(8,128)} %bitcast.11, bf16[128,128,128]{2,1,0:T(8,128)(2,1)} %bitcast.9, s32[1,128]{1,0:T(1,128)} %bitcast.13, s32[1,128]{1,0:T(1,128)} %bitcast.14, ...), custom_call_target="tpu_custom_call" | custom-call | tf_op jit(solution)/shard_map/layer/pallas_call | solution.py:725
  140.0 1.9 %write.1 = (bf16[32,4096]{1,0:T(8,128)(2,1)}, bf16[32,4096]{1,0:T(8,128)(2,1)}, f32[32,512]{1,0:T(8,128)}) custom-call(bf16[32,4096]{1,0:T(8,128)(2,1)} %get-tuple-element.9.refs_0_, bf16[32,4096]{1,0:T(8,128)(2,1)} %get-tuple-element.10.refs_1_, f32[32,512]{1,0:T(8,128)} %get-tuple-element.11.refs_2_), custom_call_target="tpu_custom_call" | custom-call | tf_op jit(solution)/shard_map/write/pallas_call | solution.py:790

commit v7 on v6

--- a/solution.py
+++ b/solution.py
@@ -643,11 +643,11 @@
     )
     z_lags = (
         (0, reduce_out), (2, reduce_merge), (3, reduce_second), (4, merge_second),
-        (6, activate), (7, gather_second), (9, gather_first), (11, gather_far),
+        (6, activate), (7, gather_second), (9, gather_first),
     )
     x_first = [u for u in range(units) if u not in Z_FIRST]
     steps = len(x_first) + 6
-    for step in range(steps):
+    for step in range(steps - 2):
         for lag, act in x_lags:
             if max(0, -lag) <= step - lag < len(x_first):
                 act(x_first[step - lag])
@@ -655,28 +655,31 @@
             for u in Z_FIRST:
                 if step == lag:
                     act(u)
-        if step == steps - 3:
-            for u in range(MID_CHUNKS):
-                gather_end(u)
-            backward_tiles(0, 0, TILE)
-            core_out(1)
-            core_out(0)
-        if step == steps - 2:
-            z_first(1)
-            y_out(0)
+    for u in range(MID_CHUNKS):
+        gather_end(u)
+    gather_first(x_first[-1])
+    backward_tiles(0, 0, 2 * share)
+    gather_far(x_first[-2])
+    for u in Z_FIRST:
+        gather_far(u)
+    backward_tiles(0, 2 * share, 2 * share)
+    core_out(1)
+    core_out(0)
+    gather_far(x_first[-1])
+    z_first(1)
+    y_out(0)
     for u in range(MID_CHUNKS, units):
         gather_end(u)
-    backward_tiles(1, 0, share)
+    backward_tiles(1, 0, 2 * share)
     y_merge(0)
-    backward_tiles(1, share, share)
-    z_then_y(1)
     backward_tiles(1, 2 * share, 2 * share)
     core_out(3)
     core_out(2)
+    z_then_y(1)
+    z_first(3)
+    y_out(2)
     y_merge(1)
     z_out(0)
-    z_first(3)
-    y_out(2)
     scaled(1)
     scaled(0)
     spread_weight(0)

time: 144 us -> 146 us (1.014)
  Pallas kernels: 141 us -> 143 us
    pallas_call x1, Pallas kernels: 139 us -> 141 us  [shards(): pl.pallas_call(kernel, out_shape=(jax.ShapeDtypeStruct((depth, nodes), BF...]
where the time goes in v7:
time: 146 us; the launch traced here: 144 us
  Pallas kernels  143 us (98%)
    pallas_call x1, Pallas kernels, shards(): pl.pallas_call(kernel, out_shape=(jax.ShapeDtypeStruct((depth, nodes), BF...  141 us

profile of v7, /device:TPU:0, one launch (start us, length us, event | category | flops | bytes accessed | tf_op | source)
XLA Modules:
  0.0 144.3 jit_solution(16600629533476877839)
XLA Ops:
  1.3 141.1 %layer.1 = (bf16[32,4096]{1,0:T(8,128)(2,1)}, bf16[32,4096]{1,0:T(8,128)(2,1)}, f32[32,512]{1,0:T(8,128)}) custom-call(bf16[32,4096]{1,0:T(8,128)(2,1)} %bitcast.10, bf16[512,512]{1,0:T(8,128)(2,1)} %w_hbm.1, s32[512,128]{1,0:T(8,128)} %bitcast.11, bf16[128,128,128]{2,1,0:T(8,128)(2,1)} %bitcast.9, s32[1,128]{1,0:T(1,128)} %bitcast.13, s32[1,128]{1,0:T(1,128)} %bitcast.14, ...), custom_call_target="tpu_custom_call" | custom-call | tf_op jit(solution)/shard_map/layer/pallas_call | solution.py:728
  142.4 1.9 %write.1 = (bf16[32,4096]{1,0:T(8,128)(2,1)}, bf16[32,4096]{1,0:T(8,128)(2,1)}, f32[32,512]{1,0:T(8,128)}) custom-call(bf16[32,4096]{1,0:T(8,128)(2,1)} %get-tuple-element.9.refs_0_, bf16[32,4096]{1,0:T(8,128)(2,1)} %get-tuple-element.10.refs_1_, f32[32,512]{1,0:T(8,128)} %get-tuple-element.11.refs_2_), custom_call_target="tpu_custom_call" | custom-call | tf_op jit(solution)/shard_map/write/pallas_call | solution.py:793
